TPU v7x, 256 devices: a whole 4x4x8 slice. The times are simulated.
256 devices in a mesh: dp: 64 (over z, x, core), tensor: 4 (over y).
Axes of the slice: x: 4, y: 4, z: 8, core: 2. Of those that a mesh axis runs over, the one named last changes fastest.
Arguments:
- rollouts: bfloat16 [24576, 9216], P('dp', 'tensor'), may hold values from -6 to 6
- send_order: int32 [64, 64], P('dp'), may hold values from 0 to 63, each once within a row
- segment_ids: int32 [64, 224], P('dp'), may hold values from 0 to 63, as said below
- offsets: int32 [64, 64], P('dp'), may hold values from 0 to 223, as said below
- ln_gain: float32 [9216], replicated, may hold values from 0.1 to 1.9
- qkv_weight: bfloat16 [9216, 3072], P('dp', 'tensor'), may hold values from -127 to 127, as said below
- qkv_scale: float32 [3072], P('tensor'), may hold values from 6.979167e-05 to 0.0022395833
- out_weight: bfloat16 [1536, 9216], P('tensor', 'dp'), may hold values from -127 to 127, as said below
- out_scale: float32 [9216], P('tensor'), may hold values from 0.00025005208 to 0.0009951052
Outputs:
- block_output: bfloat16 [14336, 9216], P('dp', 'tensor')
Inputs may be any that keep to these rules, and one draw needn't show every extreme that they name: `send_order`: each row is an ordering of the 64 responses of one owner. `segment_ids`: on every packed shard the 224 positions form 64 runs of consecutive positions, one for each received slot, each of 1 to 6 tokens; some run of every shard holds exactly 6. offsets[p, s] is the first position of slot s's run on packed shard p; the last run of every shard is one token long. `qkv_weight`: whole numbers. `out_weight`: whole numbers.
All inputs are finite; a program needn't handle non-finite values.
Results may differ from a plain program's by a relative error of at most 0.012.
The roundings to bfloat16 on the way count: a program that leaves them out, or rounds other values in their place, can miss the bound.
Values may be sent and summed in bfloat16 or wider, within the bound.
No kernel may reach another device: no remote copies, remote signals or barrier semaphores. Data moves between devices by JAX's collectives and lax.ppermute only.
A program may use at most 128 MiB of HBM per device.

v0:
```python
import jax
import jax.numpy as jnp
from jax import lax
from jax.sharding import PartitionSpec as P

HEAD = 192


norm_epsilon = 1e-05
masked_score = -1e30


def layer_norm(rows_float, ln_gain):
    row_mean = jnp.mean(rows_float, axis=1, keepdims=True)
    centered = rows_float - row_mean
    row_var = jnp.mean(centered * centered, axis=1, keepdims=True)
    return (centered * lax.rsqrt(row_var + norm_epsilon) * ln_gain).astype(jnp.bfloat16)


def softmax_rows(scores, allowed):
    scores = jnp.where(allowed, scores, masked_score)
    row_peak = jnp.max(scores, axis=1, keepdims=True)
    exponent = jnp.exp(scores - row_peak)
    return (exponent / jnp.sum(exponent, axis=1, keepdims=True)).astype(jnp.bfloat16)


def masked_attention(queries, key_rows, value_rows, segment):
    token_count = queries.shape[0]
    positions = jnp.arange(token_count, dtype=jnp.int32)
    score_scale = float(queries.shape[1]) ** (-0.5)
    scores = (
        jnp.einsum("td,ud->tu", queries, key_rows, preferred_element_type=jnp.float32) * score_scale
    )
    allowed = (segment[:, None] == segment[None, :]) & (positions[None, :] <= positions[:, None])
    weights = softmax_rows(scores, allowed)
    return jnp.dot(weights, value_rows, preferred_element_type=jnp.float32).astype(jnp.bfloat16)


def per_device(
    rollouts,
    send_order,
    segment_ids,
    offsets,
    ln_gain,
    qkv_weight,
    qkv_scale,
    out_weight,
    out_scale,
):
    response_count = send_order.shape[1]
    feature_count = rollouts.shape[1]
    longest = rollouts.shape[0] // response_count
    slot_rows = rollouts.reshape(response_count, longest, feature_count)
    outgoing = jnp.take(slot_rows, send_order[0], axis=0)
    arrived = lax.all_to_all(outgoing, "dp", split_axis=0, concat_axis=0, tiled=True)
    segment = segment_ids[0]
    token_count = segment.shape[0]
    within = jnp.clip(
        jnp.arange(token_count, dtype=jnp.int32) - offsets[0][segment], 0, longest - 1
    )
    packed = arrived.reshape(response_count * longest, feature_count)[segment * longest + within]
    gathered = lax.all_gather(packed, "tensor", axis=1, tiled=True)
    normed = layer_norm(gathered.astype(jnp.float32), ln_gain)
    projected = jnp.dot(
        normed,
        lax.all_gather(qkv_weight, "dp", axis=0, tiled=True),
        preferred_element_type=jnp.float32,
    )
    projected = (projected * qkv_scale).astype(jnp.bfloat16)
    head_size = HEAD
    group_count = projected.shape[1] // head_size - 2
    key_rows = projected[:, group_count * head_size : (group_count + 1) * head_size]
    value_rows = projected[:, (group_count + 1) * head_size :]
    outputs = []
    for member in range(group_count):
        queries = projected[:, member * head_size : (member + 1) * head_size]
        outputs.append(masked_attention(queries, key_rows, value_rows, segment))
    attended = jnp.concatenate(outputs, axis=1)
    terms = jnp.dot(
        attended,
        lax.all_gather(out_weight, "dp", axis=1, tiled=True),
        preferred_element_type=jnp.float32,
    )
    branch = lax.psum_scatter(terms, "tensor", scatter_dimension=1, tiled=True) * out_scale
    return (packed.astype(jnp.float32) + branch).astype(jnp.bfloat16)


def solution(mesh):
    in_specs = (
        P("dp", "tensor"),
        P("dp", None),
        P("dp", None),
        P("dp", None),
        P(),
        P("dp", "tensor"),
        P("tensor"),
        P("tensor", "dp"),
        P("tensor"),
    )
    out_specs = P("dp", "tensor")
    return jax.shard_map(
        per_device, mesh=mesh, in_specs=in_specs, out_specs=out_specs, check_vma=False
    )
```

profile of v0, /device:TPU:1, one launch (start us, length us, event | category | flops | bytes accessed | tf_op | source)
XLA Modules:
  0.0 412.8 jit_solution(16011695462873773744)
XLA Ops:
  6.5 0.7 fusion.36
  7.2 0.7 compare_and_fusion
  7.9 3.8 reshape.124
  11.7 2.4 gather_fusion
  14.1 1.7 broadcast_select_fusion
  15.8 13.2 %all-to-all-start = ((bf16[64,6,2304]{2,1,0:T(8,128)(2,1)}), bf16[64,6,2304]{2,1,0:T(8,128)(2,1)}, u32[]{:S(2)}, u32[]{:S(2)}) async-start(bf16[64,6,2304]{2,1,0:T(8,128)(2,1)} %broadcast_select_fusion), calls=%async_computation | async-start | bytes 4718592 | tf_op jit(solution)/shard_map/all_to_all | solution.py:55
  29.1 1.9 gather_fusion.1
  31.0 53.1 %all-to-all-done = bf16[64,6,2304]{2,1,0:T(8,128)(2,1)} async-done(((bf16[64,6,2304]{2,1,0:T(8,128)(2,1)}), bf16[64,6,2304]{2,1,0:T(8,128)(2,1)}, u32[]{:S(2)}, u32[]{:S(2)}) %all-to-all-start) | async-done | bytes 1769504 | tf_op jit(solution)/shard_map/all_to_all | solution.py:55
  84.1 2.7 reshape.125
  86.8 2.3 gather_fusion.2
  89.1 0.7 all-gather.5.cloned.1.call-update
  89.9 0.7 all-gather.7.cloned.1.call-update
  90.6 46.8 %all-gather.9.cloned.1.call-done = bf16[224,9216]{1,0:T(8,128)(2,1)} async-done(((bf16[224,2304]{1,0:T(8,128)(2,1)}), bf16[224,9216]{1,0:T(8,128)(2,1)}) %all-gather.9.cloned.1.call-update) | async-done | bytes 4128784 | tf_op jit(solution)/shard_map/all_gather | solution.py:62
  137.5 3.0 convert_reduce_fusion
  140.4 0.4 copy-done.1
  140.9 1.2 fusion.2
  142.1 92.2 %all-gather.5.cloned.1.call-done = bf16[9216,768]{1,0:T(8,128)(2,1)} async-done(((bf16[144,768]{1,0:T(8,128)(2,1)}), bf16[9216,768]{1,0:T(8,128)(2,1)}) %all-gather.5.cloned.1.call-update) | async-done | bytes 14155792 | tf_op jit(solution)/shard_map/all_gather | solution.py:66
  234.3 9.8 %fusion.13 = bf16[224,768]{1,0:T(8,128)(2,1)S(1)} fusion(bf16[9216,768]{1,0:T(8,128)(2,1)} %all-gather.5.cloned.1.call-done, bf16[224,9216]{1,0:T(8,128)(2,1)} %all-gather.9.cloned.1.call-done, f32[9216]{0:T(1024)S(1)} %copy-done.5, f32[224]{0:T(256)S(1)} %add_rsqrt_fusion, f32[224]{0:T(256)S(1)} %broadcast_multiply_fusion, f32[768]{0:T(1024)S(1)} %copy-done.6), kind=kOutput, calls=%fused_computation.17 | convolution fusion | flops 3181559808 | bytes 18670336 | tf_op jit(solution)/shard_map/dot_general | solution.py:64
  244.4 0.3 fusion.38
  245.1 0.3 convolution_convert_fusion
  245.4 70.6 %all-gather.7.cloned.1.call-done = bf16[384,9216]{0,1:T(8,128)(2,1)} async-done(((bf16[384,144]{0,1:T(8,128)(2,1)}), bf16[384,9216]{0,1:T(8,128)(2,1)}) %all-gather.7.cloned.1.call-update) | async-done | bytes 7077904 | tf_op jit(solution)/shard_map/all_gather | solution.py:81
  316.0 8.8 %fusion.21 = f32[224,9216]{1,0:T(8,128)} fusion(bf16[384,9216]{0,1:T(8,128)(2,1)} %all-gather.7.cloned.1.call-done, bf16[224,192]{1,0:T(8,128)(2,1)S(1)} %convolution_convert_fusion, bf16[224,192]{1,0:T(8,128)(2,1)S(1)} %convolution_convert_fusion.1), kind=kOutput, calls=%fused_computation.32 | convolution fusion | flops 1585790976 | bytes 15507456 | tf_op jit(solution)/shard_map/dot_general | solution.py:79
  324.9 78.6 %reduce-scatter.2.cloned.1.call-done = f32[224,2304]{1,0:T(8,128)} async-done(((f32[224,9216]{1,0:T(8,128)}), f32[224,2304]{1,0:T(8,128)}) %reduce-scatter.2.cloned.1.call-update) | async-done | bytes 2064400 | tf_op jit(solution)/shard_map/reduce_scatter | solution.py:84
  403.5 2.8 add_convert_fusion
  (30 shorter events, 0.9 us)
Async XLA Ops:
  6.5 22.5 %copy-start = (s32[1,64]{1,0:T(1,128)S(1)}, s32[1,64]{1,0:T(1,128)}, u32[]{:S(2)}) copy-start(s32[1,64]{1,0:T(1,128)} %param.12) | copy-start | bytes 772
  14.1 15.0 %copy-start.4 = (s32[1,224]{1,0:T(1,128)S(1)}, s32[1,224]{1,0:T(1,128)}, u32[]{:S(2)}) copy-start(s32[1,224]{1,0:T(1,128)} %param.11) | copy-start | bytes 2692
  15.8 68.3 %all-to-all-start = ((bf16[64,6,2304]{2,1,0:T(8,128)(2,1)}), bf16[64,6,2304]{2,1,0:T(8,128)(2,1)}, u32[]{:S(2)}, u32[]{:S(2)}) async-start(bf16[64,6,2304]{2,1,0:T(8,128)(2,1)} %broadcast_select_fusion), calls=%async_computation | async-start | bytes 4718592 | tf_op jit(solution)/shard_map/all_to_all | solution.py:55
  29.0 108.5 %all-gather.9.cloned.1.call-start = ((), (), s32[]{:S(2)}) async-start(), calls=%async_computation.5 | async-start | bytes 5160960 | tf_op jit(solution)/shard_map/all_gather | solution.py:62
  89.1 145.2 %all-gather.5.cloned.1.call-start = ((), (), s32[]{:S(2)}) async-start(), calls=%async_computation.2 | async-start | bytes 14376960 | tf_op jit(solution)/shard_map/all_gather | solution.py:66
  89.8 226.2 %all-gather.7.cloned.1.call-start = ((), (), s32[]{:S(2)}) async-start(), calls=%async_computation.3 | async-start | bytes 7188480 | tf_op jit(solution)/shard_map/all_gather | solution.py:81
  89.9 144.4 %copy-start.5 = (f32[9216]{0:T(1024)S(1)}, f32[9216]{0:T(1024)}, u32[]{:S(2)}) copy-start(f32[9216]{0:T(1024)} %param.13) | copy-start | bytes 110596
  89.9 144.4 %copy-start.6 = (f32[768]{0:T(1024)S(1)}, f32[768]{0:T(1024)}, u32[]{:S(2)}) copy-start(f32[768]{0:T(1024)} %param.15) | copy-start | bytes 9220
  90.6 312.9 %reduce-scatter.2.cloned.1.call-start = ((), (), s32[]{:S(2)}) async-start(), calls=%async_computation.4 | async-start | bytes 10321920 | tf_op jit(solution)/shard_map/reduce_scatter | solution.py:84
  137.5 3.4 copy-start.1
  324.8 78.6 %copy-start.2 = (bf16[224,2304]{1,0:T(8,128)(2,1)S(1)}, bf16[224,2304]{1,0:T(8,128)(2,1)}, u32[]{:S(2)}) copy-start(bf16[224,2304]{1,0:T(8,128)(2,1)} %gather_fusion.2) | copy-start | bytes 3096580
  324.8 78.6 %copy-start.3 = (f32[2304]{0:T(1024)S(1)}, f32[2304]{0:T(1024)}, u32[]{:S(2)}) copy-start(f32[2304]{0:T(1024)} %param.17) | copy-start | bytes 27652
Sparse Core Ops, SparseCore 0:
  89.2 48.2 all-gather.8
  140.2 94.0 all-gather.4
  237.0 78.9 all-gather.6
  325.0 78.4 reduce-scatter.1
where the time goes:
time: 413 us
  waiting for transfers between devices  343 us (83%)
  matrix products  19.8 us (5%)
  local copies, waits for them, and re-layouts  13.5 us (3%)
  starting transfers between devices  13.3 us (3%)
  between operations  13.3 us (3%)
  other arithmetic  10.3 us (2%)
    all_gather x1, waiting for transfers between devices, per_device(): lax.all_gather(qkv_weight, 'dp', axis=0, tiled=True)  92.2 us
    reduce_scatter x1, waiting for transfers between devices, per_device(): lax.psum_scatter(terms, 'tensor', scatter_dimension=1, tiled=True)  78.6 us
    all_gather x1, waiting for transfers between devices, per_device(): lax.all_gather(out_weight, 'dp', axis=1, tiled=True)  70.6 us
    all_to_all x1, waiting for transfers between devices, per_device(): lax.all_to_all(outgoing, 'dp', split_axis=0, concat_axis=0, tiled=True)  53.1 us
    all_gather x1, waiting for transfers between devices, per_device(): gathered = lax.all_gather(packed, 'tensor', axis=1, tiled=True)  46.8 us
    all_to_all x1, starting transfers between devices, per_device(): lax.all_to_all(outgoing, 'dp', split_axis=0, concat_axis=0, tiled=True)  13.2 us
    dot_general x1, matrix products, per_device(): jnp.dot(normed, lax.all_gather(qkv_weight, 'dp', axis=0, tiled=True), pre...  9.84 us
    dot_general x1, matrix products, per_device(): jnp.dot(attended, lax.all_gather(out_weight, 'dp', axis=1, tiled=True), p...  8.83 us
  transfers between devices with their start and end apart: 5, of which 5 were waited for; matrix products, arithmetic and copies ran while one was open for 4% of the time, Pallas kernels for 0%

commit v1 on v0

v1 whole, which is shorter than its diff:
```python
import jax
import jax.numpy as jnp
from jax import lax
from jax.sharding import Mesh, PartitionSpec as P

HEAD = 192
norm_epsilon = 1e-05
masked_score = -1e30
DP = ("z", "x", "c")


def layer_norm(rows_float, ln_gain):
    row_mean = jnp.mean(rows_float, axis=1, keepdims=True)
    centered = rows_float - row_mean
    row_var = jnp.mean(centered * centered, axis=1, keepdims=True)
    return (centered * lax.rsqrt(row_var + norm_epsilon) * ln_gain).astype(jnp.bfloat16)


def softmax_rows(scores, allowed):
    scores = jnp.where(allowed, scores, masked_score)
    row_peak = jnp.max(scores, axis=1, keepdims=True)
    exponent = jnp.exp(scores - row_peak)
    return (exponent / jnp.sum(exponent, axis=1, keepdims=True)).astype(jnp.bfloat16)


def masked_attention(queries, key_rows, value_rows, segment):
    token_count = queries.shape[0]
    positions = jnp.arange(token_count, dtype=jnp.int32)
    score_scale = float(queries.shape[1]) ** (-0.5)
    scores = (
        jnp.einsum("td,ud->tu", queries, key_rows, preferred_element_type=jnp.float32) * score_scale
    )
    allowed = (segment[:, None] == segment[None, :]) & (positions[None, :] <= positions[:, None])
    weights = softmax_rows(scores, allowed)
    return jnp.dot(weights, value_rows, preferred_element_type=jnp.float32).astype(jnp.bfloat16)


def shift(value, axis, size, step):
    return lax.ppermute(value, axis, [(i, (i + step) % size) for i in range(size)])


def gather_over_y(block, y_size):
    half = block.shape[0] // 2
    below = shift(block, "y", y_size, 1)
    above = shift(block, "y", y_size, -1)
    far_low = shift(below[:half], "y", y_size, 1)
    far_high = shift(above[half:], "y", y_size, -1)
    return block, below, above, jnp.concatenate([far_low, far_high], axis=0)


def per_device(sizes, rollouts, send_order, segment_ids, offsets, ln_gain,
               qkv_weight, qkv_scale, out_weight, out_scale):
    z_size, x_size, c_size, y_size = sizes
    y = lax.axis_index("y")
    per_plane = z_size // y_size
    swap = []
    for z in range(z_size):
        a, b = z // per_plane, z % per_plane
        for k in range(y_size):
            swap.append((z * y_size + k, (k * per_plane + b) * y_size + a))
    out_block = lax.ppermute(out_weight.T, ("z", "y"), swap)
    qkv_full = lax.all_gather(qkv_weight, DP, axis=0, tiled=True)
    out_full = lax.all_gather(out_block, DP, axis=0, tiled=True)

    response_count = send_order.shape[1]
    feature_count = rollouts.shape[1]
    longest = rollouts.shape[0] // response_count
    slot_rows = rollouts.reshape(response_count, longest, feature_count)
    outgoing = jnp.take(slot_rows, send_order[0], axis=0)
    arrived = lax.all_to_all(outgoing, DP, split_axis=0, concat_axis=0, tiled=True)
    segment = segment_ids[0]
    token_count = segment.shape[0]
    within = jnp.clip(
        jnp.arange(token_count, dtype=jnp.int32) - offsets[0][segment], 0, longest - 1
    )
    packed = arrived.reshape(response_count * longest, feature_count)[segment * longest + within]
    own, below, above, far = gather_over_y(packed, y_size)
    gathered = jnp.zeros((token_count, y_size * feature_count), packed.dtype)
    for step, part in ((0, own), (-1, below), (1, above), (2, far)):
        at = ((y + step) % y_size) * feature_count
        gathered = lax.dynamic_update_slice(gathered, part, (0, at))
    normed = layer_norm(gathered.astype(jnp.float32), ln_gain)
    projected = jnp.dot(normed, qkv_full, preferred_element_type=jnp.float32)
    projected = (projected * qkv_scale).astype(jnp.bfloat16)
    head_size = HEAD
    group_count = projected.shape[1] // head_size - 2
    key_rows = projected[:, group_count * head_size : (group_count + 1) * head_size]
    value_rows = projected[:, (group_count + 1) * head_size :]
    outputs = []
    for member in range(group_count):
        queries = projected[:, member * head_size : (member + 1) * head_size]
        outputs.append(masked_attention(queries, key_rows, value_rows, segment))
    attended = jnp.concatenate(outputs, axis=1)
    attended = lax.all_gather(attended, "y", axis=0, tiled=False)
    out_full = out_full.reshape(y_size, feature_count, attended.shape[2])
    branch = 0.0
    for k in range(y_size):
        branch = branch + jnp.einsum(
            "td,fd->tf", attended[k], out_full[k], preferred_element_type=jnp.float32
        )
    return (packed.astype(jnp.float32) + branch * out_scale).astype(jnp.bfloat16)


def solution(mesh):
    chips = Mesh(mesh.devices.reshape(8, 4, 2, 4), ("z", "x", "c", "y"))
    in_specs = (
        P(DP, "y"),
        P(DP, None),
        P(DP, None),
        P(DP, None),
        P(),
        P(DP, "y"),
        P("y"),
        P("y", DP),
        P("y"),
    )

    def body(*args):
        return per_device((8, 4, 2, 4), *args)

    return jax.shard_map(
        body, mesh=chips, in_specs=in_specs, out_specs=P(DP, "y"), check_vma=False
    )
```

time: 413 us -> 232 us (0.56)
  waiting for transfers between devices: 343 us -> 137 us
  starting transfers between devices: 13.3 us -> 34 us
  blocking collectives: 0 us -> 11.4 us
  other arithmetic: 10.3 us -> 5.7 us
    all_gather x3 -> x2, waiting for transfers between devices: 210 us -> 39.6 us  [the longest x1 39.6 us: per_device(): out_full = lax.all_gather(out_block, DP, axis=0, tiled=True)]
    reduce_scatter x1 -> x0, waiting for transfers between devices: 78.6 us -> none  [per_device(): lax.psum_scatter(terms, 'tensor', scatter_dimension=1, tiled=True)]
    ppermute x0 -> x5, waiting for transfers between devices: none -> 29.3 us  [the longest x4 29.3 us: shift(): lax.ppermute(value, axis, [(i, (i + step) % size) for i in range(size)])]
    all_to_all x1, waiting for transfers between devices: 53.1 us -> 66.9 us  [per_device(): lax.all_to_all(outgoing, DP, split_axis=0, concat_axis=0, tiled=True)]
    all_to_all x1, starting transfers between devices: 13.2 us -> 26.6 us  [per_device(): lax.all_to_all(outgoing, DP, split_axis=0, concat_axis=0, tiled=True)]
    all_gather x0 -> x1, blocking collectives: none -> 11.4 us  [per_device(): attended = lax.all_gather(attended, 'y', axis=0, tiled=False)]
    ppermute x0 -> x5, starting transfers between devices: none -> 7.37 us  [the longest x4 5.82 us: shift(): lax.ppermute(value, axis, [(i, (i + step) % size) for i in range(size)])]
    dot_general x2 -> x5, matrix products: 18.7 us -> 17.2 us  [the longest x1 9.9 us: per_device(): projected = jnp.dot(normed, qkv_full, preferred_element_type=jnp.float32)]
  transfers between devices with their start and end apart: 5 -> 8, of which waited for: 5 -> 4; matrix products, arithmetic and copies ran while one was open for 4% -> 12% of each run, Pallas kernels for 0% -> 0%
where the time goes in v1:
time: 232 us
  waiting for transfers between devices  137 us (59%)
  starting transfers between devices  34 us (15%)
  matrix products  18.4 us (8%)
  between operations  13.7 us (6%)
  local copies, waits for them, and re-layouts  12.4 us (5%)
  blocking collectives  11.4 us (5%)
  other arithmetic  5.7 us (2%)
    all_to_all x1, waiting for transfers between devices, per_device(): lax.all_to_all(outgoing, DP, split_axis=0, concat_axis=0, tiled=True)  66.9 us
    all_gather x1, waiting for transfers between devices, per_device(): out_full = lax.all_gather(out_block, DP, axis=0, tiled=True)  39.6 us
    ppermute x4, waiting for transfers between devices, shift(): lax.ppermute(value, axis, [(i, (i + step) % size) for i in range(size)])  29.3 us
    all_to_all x1, starting transfers between devices, per_device(): lax.all_to_all(outgoing, DP, split_axis=0, concat_axis=0, tiled=True)  26.6 us
    all_gather x1, blocking collectives, per_device(): attended = lax.all_gather(attended, 'y', axis=0, tiled=False)  11.4 us
    dot_general x1, matrix products, per_device(): projected = jnp.dot(normed, qkv_full, preferred_element_type=jnp.float32)  9.9 us
    dot_general x4, matrix products, per_device(): jnp.einsum('td,fd->tf', attended[k], out_full[k], preferred_element_type=...  7.32 us
    ppermute x4, starting transfers between devices, shift(): lax.ppermute(value, axis, [(i, (i + step) % size) for i in range(size)])  5.82 us
  transfers between devices with their start and end apart: 8, of which 4 were waited for; matrix products, arithmetic and copies ran while one was open for 12% of the time, Pallas kernels for 0%

profile of v1, /device:TPU:1, one launch (start us, length us, event | category | flops | bytes accessed | tf_op | source)
XLA Modules:
  0.0 232.1 jit_solution(481846609818464751)
XLA Ops:
  6.5 0.7 all-gather.4.cloned.1.call-update
  7.3 1.6 collective-permute-start.4
  8.9 0.6 copy-done.3
  9.5 2.6 %reshape.133 = bf16[64,6,2304]{2,1,0:T(8,128)(2,1)S(1)} reshape(bf16[384,2304]{1,0:T(8,128)(2,1)} %param.9) | data formatting | bytes 3538944 | tf_op jit(solution)/shard_map/reshape | solution.py:68
  12.2 2.2 gather_fusion
  14.3 3.5 %broadcast_select_fusion = bf16[64,6,2304]{2,1,0:T(8,128)(2,1)} fusion(bf16[64,6,2304]{2,1,0:T(8,128)(2,1)} %gather_fusion, pred[64]{0:T(512)(128)(4,1)S(1)} %compare_and_fusion), kind=kLoop, calls=%fused_computation.20 | loop fusion | flops 884736 | bytes 3539008 | tf_op jit(solution)/shard_map/jit(_take)/select_n | solution.py:69
  17.8 26.6 %all-to-all-start = ((bf16[64,6,2304]{2,1,0:T(8,128)(2,1)}), bf16[64,6,2304]{2,1,0:T(8,128)(2,1)}, u32[]{:S(2)}, u32[]{:S(2)}) async-start(bf16[64,6,2304]{2,1,0:T(8,128)(2,1)} %broadcast_select_fusion), calls=%async_computation | async-start | bytes 4718592 | tf_op jit(solution)/shard_map/all_to_all | solution.py:70
  44.5 1.9 gather_fusion.1
  46.4 66.9 %all-to-all-done = bf16[64,6,2304]{2,1,0:T(8,128)(2,1)} async-done(((bf16[64,6,2304]{2,1,0:T(8,128)(2,1)}), bf16[64,6,2304]{2,1,0:T(8,128)(2,1)}, u32[]{:S(2)}, u32[]{:S(2)}) %all-to-all-start) | async-done | bytes 1769504 | tf_op jit(solution)/shard_map/all_to_all | solution.py:70
  113.3 2.7 %reshape.134 = bf16[384,2304]{1,0:T(8,128)(2,1)S(1)} reshape(bf16[64,6,2304]{2,1,0:T(8,128)(2,1)} %all-to-all-done) | data formatting | bytes 3538944 | tf_op jit(solution)/shard_map/reshape | solution.py:76
  116.0 1.3 gather_fusion.2
  117.6 2.5 %collective-permute-start.1 = (bf16[224,2304]{1,0:T(8,128)(2,1)S(1)}, bf16[224,2304]{1,0:T(8,128)(2,1)S(1)}, u32[]{:S(2)}, u32[]{:S(2)}) collective-permute-start(bf16[224,2304]{1,0:T(8,128)(2,1)S(1)} %gather_fusion.2), channel_id=1, source_target_pairs={{0,3},{1,0},{2,1},{3,2},{4,7},{5,4},{6,5},{7,6},{8,11},{9,8},{10,9... | collective-permute-start | bytes 3096584 | tf_op jit(solution)/shard_map/ppermute | solution.py:39
  120.8 20.6 %collective-permute-done = bf16[224,2304]{1,0:T(8,128)(2,1)S(1)} collective-permute-done((bf16[224,2304]{1,0:T(8,128)(2,1)S(1)}, bf16[224,2304]{1,0:T(8,128)(2,1)S(1)}, u32[]{:S(2)}, u32[]{:S(2)}) %collective-permute-start) | collective-permute-done | bytes 1032224 | tf_op jit(solution)/shard_map/ppermute | solution.py:39
  141.5 2.9 %collective-permute-start.3 = (bf16[112,2304]{1,0:T(8,128)(2,1)S(1)}, bf16[112,2304]{1,0:T(8,128)(2,1)S(1)}, u32[]{:S(2)}, u32[]{:S(2)}) collective-permute-start(bf16[112,2304]{1,0:T(8,128)(2,1)S(1)} %slice.71), channel_id=1, source_target_pairs={{0,3},{1,0},{2,1},{3,2},{4,7},{5,4},{6,5},{7,6},{8,11},{9,8},{10,9... | collective-permute-start | bytes 1548296 | tf_op jit(solution)/shard_map/ppermute | solution.py:39
  144.7 8.7 %collective-permute-done.2 = bf16[112,2304]{1,0:T(8,128)(2,1)S(1)} collective-permute-done((bf16[112,2304]{1,0:T(8,128)(2,1)S(1)}, bf16[112,2304]{1,0:T(8,128)(2,1)S(1)}, u32[]{:S(2)}, u32[]{:S(2)}) %collective-permute-start.2) | collective-permute-done | bytes 516128 | tf_op jit(solution)/shard_map/ppermute | solution.py:39
  153.5 0.7 convert_reduce_fusion
  154.2 1.2 fusion.2
  155.5 9.9 %fusion.25 = bf16[224,768]{1,0:T(8,128)(2,1)S(1)} fusion(bf16[9216,768]{1,0:T(8,128)(2,1)} %all-gather.4.cloned.1.call-done, bf16[224,9216]{1,0:T(8,128)(2,1)} %copy-done.1, f32[9216]{0:T(1024)S(1)} %copy-done.6, f32[224]{0:T(256)S(1)} %add_rsqrt_fusion, f32[224]{0:T(256)S(1)} %broadcast_multiply_fusion, f32[768]{0:T(1024)S(1)} %copy-done.7), kind=kOutput, calls=%fused_computation.29 | convolution fusion | flops 3181559808 | bytes 18670336 | tf_op jit(solution)/shard_map/dot_general | solution.py:83
  166.9 11.4 %all-gather = bf16[896,384]{1,0:T(8,128)(2,1)S(1)} all-gather(bf16[224,384]{1,0:T(8,128)(2,1)S(1)} %copy.10), channel_id=2, replica_groups=mesh['z'=8,'x'=4,'c'=2,'y'=4] {'y'}, dimensions={0}, use_global_device_ids=true | all-gather | bytes 860160 | tf_op jit(solution)/shard_map/all_gather | solution.py:94
  178.3 39.6 %all-gather.6.cloned.1.call-done = bf16[9216,384]{1,0:T(8,128)(2,1)} async-done(((bf16[144,384]{1,0:T(8,128)(2,1)}), bf16[9216,384]{1,0:T(8,128)(2,1)}) %all-gather.6.cloned.1.call-update) | async-done | bytes 7077904 | tf_op jit(solution)/shard_map/all_gather | solution.py:63
  217.9 2.4 %fusion.17 = f32[224,2304]{1,0:T(8,128)S(1)} fusion(bf16[9216,384]{1,0:T(8,128)(2,1)} %all-gather.6.cloned.1.call-done, bf16[896,384]{1,0:T(8,128)(2,1)S(1)} %all-gather), kind=kOutput, calls=%fused_computation.23 | convolution fusion | flops 396361728 | bytes 4005888 | tf_op jit(solution)/shard_map/td,fd->tf/dot_general | solution.py:98
  220.3 2.4 %fusion.19 = f32[224,2304]{1,0:T(8,128)S(1)} fusion(bf16[9216,384]{1,0:T(8,128)(2,1)} %all-gather.6.cloned.1.call-done, bf16[896,384]{1,0:T(8,128)(2,1)S(1)} %all-gather), kind=kOutput, calls=%fused_computation.25 | convolution fusion | flops 396361728 | bytes 4005888 | tf_op jit(solution)/shard_map/td,fd->tf/dot_general | solution.py:98
  222.7 0.8 fusion.15
  223.4 1.8 fusion.14
  (50 shorter events, 3.0 us)
Async XLA Ops:
  6.5 37.9 %copy-start = (s32[1,64]{1,0:T(1,128)S(1)}, s32[1,64]{1,0:T(1,128)}, u32[]{:S(2)}) copy-start(s32[1,64]{1,0:T(1,128)} %param.12) | copy-start | bytes 772
  6.5 5.6 %copy-start.8 = (s32[1,64]{1,0:T(1,128)S(1)}, s32[1,64]{1,0:T(1,128)}, u32[]{:S(2)}) copy-start(s32[1,64]{1,0:T(1,128)} %param.10) | copy-start | bytes 772
  6.5 148.9 %all-gather.4.cloned.1.call-start = ((), (), s32[]{:S(2)}) async-start(), calls=%async_computation.1 | async-start | bytes 14376960 | tf_op jit(solution)/shard_map/all_gather | solution.py:62
  7.3 210.6 %all-gather.6.cloned.1.call-start = ((), (), s32[]{:S(2)}) async-start(), calls=%async_computation.2 | async-start | bytes 7188480 | tf_op jit(solution)/shard_map/all_gather | solution.py:63
  7.3 1.6 collective-permute-start.4
  8.9 0.6 copy-start.3
  14.3 30.1 %copy-start.5 = (s32[1,224]{1,0:T(1,128)S(1)}, s32[1,224]{1,0:T(1,128)}, u32[]{:S(2)}) copy-start(s32[1,224]{1,0:T(1,128)} %param.11) | copy-start | bytes 2692
  17.8 95.5 %all-to-all-start = ((bf16[64,6,2304]{2,1,0:T(8,128)(2,1)}), bf16[64,6,2304]{2,1,0:T(8,128)(2,1)}, u32[]{:S(2)}, u32[]{:S(2)}) async-start(bf16[64,6,2304]{2,1,0:T(8,128)(2,1)} %broadcast_select_fusion), calls=%async_computation | async-start | bytes 4718592 | tf_op jit(solution)/shard_map/all_to_all | solution.py:70
  117.3 24.0 %collective-permute-start = (bf16[224,2304]{1,0:T(8,128)(2,1)S(1)}, bf16[224,2304]{1,0:T(8,128)(2,1)S(1)}, u32[]{:S(2)}, u32[]{:S(2)}) collective-permute-start(bf16[224,2304]{1,0:T(8,128)(2,1)S(1)} %gather_fusion.2), channel_id=1, source_target_pairs={{0,1},{1,2},{2,3},{3,0},{4,5},{5,6},{6,7},{7,4},{8,9},{9,10},{10,1... | collective-permute-start | bytes 3096584 | tf_op jit(solution)/shard_map/ppermute | solution.py:39
  117.6 23.8 %collective-permute-start.1 = (bf16[224,2304]{1,0:T(8,128)(2,1)S(1)}, bf16[224,2304]{1,0:T(8,128)(2,1)S(1)}, u32[]{:S(2)}, u32[]{:S(2)}) collective-permute-start(bf16[224,2304]{1,0:T(8,128)(2,1)S(1)} %gather_fusion.2), channel_id=1, source_target_pairs={{0,3},{1,0},{2,1},{3,2},{4,7},{5,4},{6,5},{7,6},{8,11},{9,8},{10,9... | collective-permute-start | bytes 3096584 | tf_op jit(solution)/shard_map/ppermute | solution.py:39
  141.4 12.0 %collective-permute-start.2 = (bf16[112,2304]{1,0:T(8,128)(2,1)S(1)}, bf16[112,2304]{1,0:T(8,128)(2,1)S(1)}, u32[]{:S(2)}, u32[]{:S(2)}) collective-permute-start(bf16[112,2304]{1,0:T(8,128)(2,1)S(1)} %slice.70), channel_id=1, source_target_pairs={{0,1},{1,2},{2,3},{3,0},{4,5},{5,6},{6,7},{7,4},{8,9},{9,10},{10,1... | collective-permute-start | bytes 1548296 | tf_op jit(solution)/shard_map/ppermute | solution.py:39
  141.5 11.9 %collective-permute-start.3 = (bf16[112,2304]{1,0:T(8,128)(2,1)S(1)}, bf16[112,2304]{1,0:T(8,128)(2,1)S(1)}, u32[]{:S(2)}, u32[]{:S(2)}) collective-permute-start(bf16[112,2304]{1,0:T(8,128)(2,1)S(1)} %slice.71), channel_id=1, source_target_pairs={{0,3},{1,0},{2,1},{3,2},{4,7},{5,4},{6,5},{7,6},{8,11},{9,8},{10,9... | collective-permute-start | bytes 1548296 | tf_op jit(solution)/shard_map/ppermute | solution.py:39
  153.5 2.0 copy-start.1
  153.5 2.0 copy-start.6
  153.5 2.0 copy-start.7
  217.9 4.8 %copy-start.2 = (bf16[9216,384]{1,0:T(8,128)(2,1)S(1)}, bf16[9216,384]{1,0:T(8,128)(2,1)}, u32[]{:S(2)}) copy-start(bf16[9216,384]{1,0:T(8,128)(2,1)} %all-gather.6.cloned.1.call-done) | copy-start | bytes 21233668
  220.3 3.2 %copy-start.4 = (f32[2304]{0:T(1024)S(1)}, f32[2304]{0:T(1024)}, u32[]{:S(2)}) copy-start(f32[2304]{0:T(1024)} %param.17) | copy-start | bytes 27652
Sparse Core Ops, SparseCore 0:
  10.1 125.5 all-gather.3
  138.4 79.3 all-gather.5

commit v2 on v1

--- a/solution.py
+++ b/solution.py
@@ -59,26 +59,35 @@
         for k in range(y_size):
             swap.append((z * y_size + k, (k * per_plane + b) * y_size + a))
     out_block = lax.ppermute(out_weight.T, ("z", "y"), swap)
-    qkv_full = lax.all_gather(qkv_weight, DP, axis=0, tiled=True)
-    out_full = lax.all_gather(out_block, DP, axis=0, tiled=True)
+    qkv_cols = qkv_weight.shape[1]
+    both = jnp.concatenate([qkv_weight, out_block], axis=1)
+    both = lax.all_gather(both, DP, axis=0, tiled=True)
+    qkv_full, out_full = both[:, :qkv_cols], both[:, qkv_cols:]
 
     response_count = send_order.shape[1]
     feature_count = rollouts.shape[1]
     longest = rollouts.shape[0] // response_count
-    slot_rows = rollouts.reshape(response_count, longest, feature_count)
-    outgoing = jnp.take(slot_rows, send_order[0], axis=0)
-    arrived = lax.all_to_all(outgoing, DP, split_axis=0, concat_axis=0, tiled=True)
     segment = segment_ids[0]
     token_count = segment.shape[0]
     within = jnp.clip(
         jnp.arange(token_count, dtype=jnp.int32) - offsets[0][segment], 0, longest - 1
     )
-    packed = arrived.reshape(response_count * longest, feature_count)[segment * longest + within]
-    own, below, above, far = gather_over_y(packed, y_size)
-    gathered = jnp.zeros((token_count, y_size * feature_count), packed.dtype)
-    for step, part in ((0, own), (-1, below), (1, above), (2, far)):
-        at = ((y + step) % y_size) * feature_count
-        gathered = lax.dynamic_update_slice(gathered, part, (0, at))
+    take_rows = segment * longest + within
+    gathered = jnp.zeros((token_count, y_size * feature_count), rollouts.dtype)
+    halves = []
+    half_count = feature_count // 2
+    for half in range(2):
+        slot_rows = rollouts[:, half * half_count : (half + 1) * half_count]
+        slot_rows = slot_rows.reshape(response_count, longest, half_count)
+        outgoing = jnp.take(slot_rows, send_order[0], axis=0)
+        arrived = lax.all_to_all(outgoing, DP, split_axis=0, concat_axis=0, tiled=True)
+        part = arrived.reshape(response_count * longest, half_count)[take_rows]
+        halves.append(part)
+        own, below, above, far = gather_over_y(part, y_size)
+        for step, piece in ((0, own), (-1, below), (1, above), (2, far)):
+            at = ((y + step) % y_size) * feature_count + half * half_count
+            gathered = lax.dynamic_update_slice(gathered, piece, (0, at))
+    packed = jnp.concatenate(halves, axis=1)
     normed = layer_norm(gathered.astype(jnp.float32), ln_gain)
     projected = jnp.dot(normed, qkv_full, preferred_element_type=jnp.float32)
     projected = (projected * qkv_scale).astype(jnp.bfloat16)

time: 232 us -> 212 us (0.914)
  waiting for transfers between devices: 137 us -> 59.9 us
  blocking collectives: 11.4 us -> 79 us
  starting transfers between devices: 34 us -> 19.3 us
  matrix products: 18.4 us -> 21 us
    all_to_all x0 -> x1, blocking collectives: none -> 67.6 us  [per_device(): lax.all_to_all(outgoing, DP, split_axis=0, concat_axis=0, tiled=True)]
    all_to_all x1, waiting for transfers between devices: 66.9 us -> 35 us  [per_device(): lax.all_to_all(outgoing, DP, split_axis=0, concat_axis=0, tiled=True)]
    all_gather x2 -> x1, waiting for transfers between devices: 39.6 us -> 13.1 us  [per_device(): both = lax.all_gather(both, DP, axis=0, tiled=True)]
    all_to_all x1, starting transfers between devices: 26.6 us -> 6.3 us  [per_device(): lax.all_to_all(outgoing, DP, split_axis=0, concat_axis=0, tiled=True)]
    ppermute x4 -> x8, waiting for transfers between devices: 29.3 us -> 11.8 us  [shift(): lax.ppermute(value, axis, [(i, (i + step) % size) for i in range(size)])]
    ppermute x4 -> x8, starting transfers between devices: 5.82 us -> 11.3 us  [shift(): lax.ppermute(value, axis, [(i, (i + step) % size) for i in range(size)])]
    reshape x2 -> x4, local copies, waits for them, and re-layouts: 5.31 us -> 1.16 us  [the longest x2 0.58 us: per_device(): part = arrived.reshape(response_count * longest, half_count)[take_rows]]
    dot_general x4, matrix products: 7.32 us -> 10 us  [per_device(): jnp.einsum('td,fd->tf', attended[k], out_full[k], preferred_element_type=...]
  transfers between devices with their start and end apart: 8 -> 11, of which waited for: 4 -> 5; matrix products, arithmetic and copies ran while one was open for 12% -> 7% of each run, Pallas kernels for 0% -> 0%
where the time goes in v2:
time: 212 us; the launch traced here: 210 us
  blocking collectives  79 us (37%)
  waiting for transfers between devices  59.9 us (28%)
  matrix products  21 us (10%)
  starting transfers between devices  19.3 us (9%)
  between operations  13.8 us (7%)
  local copies, waits for them, and re-layouts  11.7 us (6%)
  other arithmetic  5.38 us (3%)
    all_to_all x1, blocking collectives, per_device(): lax.all_to_all(outgoing, DP, split_axis=0, concat_axis=0, tiled=True)  67.6 us
    all_to_all x1, waiting for transfers between devices, per_device(): lax.all_to_all(outgoing, DP, split_axis=0, concat_axis=0, tiled=True)  35 us
    all_gather x1, waiting for transfers between devices, per_device(): both = lax.all_gather(both, DP, axis=0, tiled=True)  13.1 us
    ppermute x8, waiting for transfers between devices, shift(): lax.ppermute(value, axis, [(i, (i + step) % size) for i in range(size)])  11.8 us
    all_gather x1, blocking collectives, per_device(): attended = lax.all_gather(attended, 'y', axis=0, tiled=False)  11.5 us
    ppermute x8, starting transfers between devices, shift(): lax.ppermute(value, axis, [(i, (i + step) % size) for i in range(size)])  11.3 us
    dot_general x4, matrix products, per_device(): jnp.einsum('td,fd->tf', attended[k], out_full[k], preferred_element_type=...  10 us
    dot_general x1, matrix products, per_device(): projected = jnp.dot(normed, qkv_full, preferred_element_type=jnp.float32)  9.84 us
  transfers between devices with their start and end apart: 11, of which 5 were waited for; matrix products, arithmetic and copies ran while one was open for 7% of the time, Pallas kernels for 0%

profile of v2, /device:TPU:1, one launch (start us, length us, event | category | flops | bytes accessed | tf_op | source)
XLA Modules:
  0.0 210.1 jit_solution(7696127669704833680)
XLA Ops:
  6.5 1.7 collective-permute-start.8
  8.2 1.7 pad_maximum_fusion
  9.9 1.6 fusion.49
  13.6 1.4 broadcast_select_fusion
  15.1 67.6 %all_to_all.10 = bf16[64,6,1152]{2,1,0:T(8,128)(2,1)S(1)} all-to-all(bf16[64,6,1152]{2,1,0:T(8,128)(2,1)S(1)} %get-tuple-element.9), channel_id=1, replica_groups=mesh['z'=8,'x'=4,'c'=2,'y'=4] {'z','x','c'}, dimensions={0} | all-to-all | bytes 1769472 | tf_op jit(solution)/shard_map/all_to_all | solution.py:83
  82.6 6.3 %all-to-all-start.1 = ((bf16[64,6,1152]{2,1,0:T(8,128)(2,1)}), bf16[64,6,1152]{2,1,0:T(8,128)(2,1)S(1)}, u32[]{:S(2)}, u32[]{:S(2)}) async-start(bf16[64,6,1152]{2,1,0:T(8,128)(2,1)} %get-tuple-element.8), calls=%async_computation.1 | async-start | bytes 2359296 | tf_op jit(solution)/shard_map/all_to_all | solution.py:83
  89.0 1.9 gather_fusion
  93.5 1.6 collective-permute-start.1
  95.1 35.0 %all-to-all-done.1 = bf16[64,6,1152]{2,1,0:T(8,128)(2,1)S(1)} async-done(((bf16[64,6,1152]{2,1,0:T(8,128)(2,1)}), bf16[64,6,1152]{2,1,0:T(8,128)(2,1)S(1)}, u32[]{:S(2)}, u32[]{:S(2)}) %all-to-all-start.1) | async-done | bytes 884768 | tf_op jit(solution)/shard_map/all_to_all | solution.py:83
  130.4 1.2 gather_fusion.2
  132.5 1.8 collective-permute-start.5
  136.0 2.7 %collective-permute-start.3 = (bf16[112,1152]{1,0:T(8,128)(2,1)S(1)}, bf16[112,1152]{1,0:T(8,128)(2,1)S(1)}, u32[]{:S(2)}, u32[]{:S(2)}) collective-permute-start(bf16[112,1152]{1,0:T(8,128)(2,1)S(1)} %slice.100), channel_id=1, source_target_pairs={{0,3},{1,0},{2,1},{3,2},{4,7},{5,4},{6,5},{7,6},{8,11},{9,8},{10,9... | collective-permute-start | bytes 774152 | tf_op jit(solution)/shard_map/ppermute | solution.py:39
  138.7 5.4 %collective-permute-done.4 = bf16[224,1152]{1,0:T(8,128)(2,1)S(1)} collective-permute-done((bf16[224,1152]{1,0:T(8,128)(2,1)S(1)}, bf16[224,1152]{1,0:T(8,128)(2,1)S(1)}, u32[]{:S(2)}, u32[]{:S(2)}) %collective-permute-start.4) | collective-permute-done | bytes 516128 | tf_op jit(solution)/shard_map/ppermute | solution.py:39
  144.3 2.9 %collective-permute-start.7 = (bf16[112,1152]{1,0:T(8,128)(2,1)S(1)}, bf16[112,1152]{1,0:T(8,128)(2,1)S(1)}, u32[]{:S(2)}, u32[]{:S(2)}) collective-permute-start(bf16[112,1152]{1,0:T(8,128)(2,1)S(1)} %slice.102), channel_id=1, source_target_pairs={{0,3},{1,0},{2,1},{3,2},{4,7},{5,4},{6,5},{7,6},{8,11},{9,8},{10,9... | collective-permute-start | bytes 774152 | tf_op jit(solution)/shard_map/ppermute | solution.py:39
  148.4 1.2 collective-permute-done.2
  150.0 5.2 %collective-permute-done.6 = bf16[112,1152]{1,0:T(8,128)(2,1)S(1)} collective-permute-done((bf16[112,1152]{1,0:T(8,128)(2,1)S(1)}, bf16[112,1152]{1,0:T(8,128)(2,1)S(1)}, u32[]{:S(2)}, u32[]{:S(2)}) %collective-permute-start.6) | collective-permute-done | bytes 258080 | tf_op jit(solution)/shard_map/ppermute | solution.py:39
  156.0 1.2 fusion.4
  157.3 13.1 %all-gather.3.cloned.1.call-done = bf16[9216,1152]{1,0:T(8,128)(2,1)} async-done(((bf16[144,1152]{1,0:T(8,128)(2,1)}), bf16[9216,1152]{1,0:T(8,128)(2,1)}) %all-gather.3.cloned.1.call-update) | async-done | bytes 21233680 | tf_op jit(solution)/shard_map/all_gather | solution.py:64
  170.4 9.8 %fusion.24 = bf16[224,768]{1,0:T(8,128)(2,1)S(1)} fusion(bf16[9216,1152]{1,0:T(8,128)(2,1)} %all-gather.3.cloned.1.call-done, bf16[224,9216]{1,0:T(8,128)(2,1)} %copy-done.1, f32[9216]{0:T(1024)S(1)} %copy-done.4, f32[224]{0:T(256)S(1)} %add_rsqrt_fusion, f32[224]{0:T(256)S(1)} %broadcast_multiply_fusion, f32[768]{0:T(1024)S(1)} %copy-done.5), kind=kOutput, calls=%fused_computation.29 | convolution fusion | flops 3181559808 | bytes 18670336 | tf_op jit(solution)/shard_map/dot_general | solution.py:92
  181.7 11.5 %all-gather = bf16[896,384]{1,0:T(8,128)(2,1)S(1)} all-gather(bf16[224,384]{1,0:T(8,128)(2,1)S(1)} %copy.10), channel_id=2, replica_groups=mesh['z'=8,'x'=4,'c'=2,'y'=4] {'y'}, dimensions={0}, use_global_device_ids=true | all-gather | bytes 860160 | tf_op jit(solution)/shard_map/all_gather | solution.py:103
  193.2 2.2 %fusion.16 = f32[224,2304]{1,0:T(8,128)S(1)} fusion(bf16[9216,1152]{1,0:T(8,128)(2,1)} %all-gather.3.cloned.1.call-done, bf16[896,384]{1,0:T(8,128)(2,1)S(1)} %all-gather), kind=kOutput, calls=%fused_computation.25 | convolution fusion | flops 396361728 | bytes 4005888 | tf_op jit(solution)/shard_map/td,fd->tf/dot_general | solution.py:107
  195.4 2.3 %convolution_add_fusion.2 = f32[224,2304]{1,0:T(8,128)S(1)} fusion(f32[224,2304]{1,0:T(8,128)S(1)} %fusion.16, bf16[9216,1152]{1,0:T(8,128)(2,1)} %all-gather.3.cloned.1.call-done, bf16[896,384]{1,0:T(8,128)(2,1)S(1)} %all-gather), kind=kOutput, calls=%fused_computation.21 | convolution fusion | flops 396877824 | bytes 6070272 | tf_op jit(solution)/shard_map/td,fd->tf/dot_general | solution.py:107
  197.7 2.3 %convolution_add_fusion.1 = f32[224,2304]{1,0:T(8,128)S(1)} fusion(f32[224,2304]{1,0:T(8,128)S(1)} %convolution_add_fusion.2, bf16[9216,1152]{1,0:T(8,128)(2,1)} %all-gather.3.cloned.1.call-done, bf16[896,384]{1,0:T(8,128)(2,1)S(1)} %all-gather), kind=kOutput, calls=%fused_computation.20 | convolution fusion | flops 396877824 | bytes 6070272 | tf_op jit(solution)/shard_map/td,fd->tf/dot_general | solution.py:107
  200.0 3.3 %fusion.13 = bf16[224,2304]{1,0:T(8,128)(2,1)} fusion(f32[224,2304]{1,0:T(8,128)S(1)} %convolution_add_fusion.1, bf16[9216,1152]{1,0:T(8,128)(2,1)} %all-gather.3.cloned.1.call-done, bf16[224,1152]{1,0:T(8,128)(2,1)S(1)} %gather_fusion.2, bf16[224,1152]{1,0:T(8,128)(2,1)S(1)} %gather_fusion.1, f32[2304]{0:T(1024)S(1)} %copy-done.2, ...), kind=kOutput, calls=%fused_computation.22 | convolution fusion | flops 400490496 | bytes 6082560 | tf_op jit(solution)/shard_map/td,fd->tf/dot_general | solution.py:107
  (64 shorter events, 11.5 us)
Async XLA Ops:
  6.5 82.5 %copy-start = (s32[1,64]{1,0:T(1,128)S(1)}, s32[1,64]{1,0:T(1,128)}, u32[]{:S(2)}) copy-start(s32[1,64]{1,0:T(1,128)} %param.14) | copy-start | bytes 772
  6.5 163.8 %all-gather.3.cloned.1.call-start = ((), (), s32[]{:S(2)}) async-start(), calls=%async_computation.2 | async-start | bytes 21565440 | tf_op jit(solution)/shard_map/all_gather | solution.py:64
  6.5 1.7 collective-permute-start.8
  9.9 2.2 %copy-start.6 = (s32[1,64]{1,0:T(1,128)S(1)}, s32[1,64]{1,0:T(1,128)}, u32[]{:S(2)}) copy-start(s32[1,64]{1,0:T(1,128)} %param.12) | copy-start | bytes 772
  13.6 75.3 %copy-start.3 = (s32[1,224]{1,0:T(1,128)S(1)}, s32[1,224]{1,0:T(1,128)}, u32[]{:S(2)}) copy-start(s32[1,224]{1,0:T(1,128)} %param.13) | copy-start | bytes 2692
  82.6 47.5 %all-to-all-start.1 = ((bf16[64,6,1152]{2,1,0:T(8,128)(2,1)}), bf16[64,6,1152]{2,1,0:T(8,128)(2,1)S(1)}, u32[]{:S(2)}, u32[]{:S(2)}) async-start(bf16[64,6,1152]{2,1,0:T(8,128)(2,1)} %get-tuple-element.8), calls=%async_computation.1 | async-start | bytes 2359296 | tf_op jit(solution)/shard_map/all_to_all | solution.py:83
  92.4 42.5 %collective-permute-start = (bf16[224,1152]{1,0:T(8,128)(2,1)S(1)}, bf16[224,1152]{1,0:T(8,128)(2,1)S(1)}, u32[]{:S(2)}, u32[]{:S(2)}) collective-permute-start(bf16[224,1152]{1,0:T(8,128)(2,1)S(1)} %gather_fusion.1), channel_id=1, source_target_pairs={{0,1},{1,2},{2,3},{3,0},{4,5},{5,6},{6,7},{7,4},{8,9},{9,10},{10,1... | collective-permute-start | bytes 1548296 | tf_op jit(solution)/shard_map/ppermute | solution.py:39
  93.5 41.5 %collective-permute-start.1 = (bf16[224,1152]{1,0:T(8,128)(2,1)S(1)}, bf16[224,1152]{1,0:T(8,128)(2,1)}, u32[]{:S(2)}, u32[]{:S(2)}) collective-permute-start(bf16[224,1152]{1,0:T(8,128)(2,1)S(1)} %gather_fusion.1), channel_id=1, source_target_pairs={{0,3},{1,0},{2,1},{3,2},{4,7},{5,4},{6,5},{7,6},{8,11},{9,8},{10,9... | collective-permute-start | bytes 1548296 | tf_op jit(solution)/shard_map/ppermute | solution.py:39
  131.6 12.5 %collective-permute-start.4 = (bf16[224,1152]{1,0:T(8,128)(2,1)S(1)}, bf16[224,1152]{1,0:T(8,128)(2,1)S(1)}, u32[]{:S(2)}, u32[]{:S(2)}) collective-permute-start(bf16[224,1152]{1,0:T(8,128)(2,1)S(1)} %gather_fusion.2), channel_id=1, source_target_pairs={{0,1},{1,2},{2,3},{3,0},{4,5},{5,6},{6,7},{7,4},{8,9},{9,10},{10,1... | collective-permute-start | bytes 1548296 | tf_op jit(solution)/shard_map/ppermute | solution.py:39
  132.5 11.7 %collective-permute-start.5 = (bf16[224,1152]{1,0:T(8,128)(2,1)S(1)}, bf16[224,1152]{1,0:T(8,128)(2,1)S(1)}, u32[]{:S(2)}, u32[]{:S(2)}) collective-permute-start(bf16[224,1152]{1,0:T(8,128)(2,1)S(1)} %gather_fusion.2), channel_id=1, source_target_pairs={{0,3},{1,0},{2,1},{3,2},{4,7},{5,4},{6,5},{7,6},{8,11},{9,8},{10,9... | collective-permute-start | bytes 1548296 | tf_op jit(solution)/shard_map/ppermute | solution.py:39
  134.9 14.7 %collective-permute-start.2 = (bf16[112,1152]{1,0:T(8,128)(2,1)S(1)}, bf16[112,1152]{1,0:T(8,128)(2,1)S(1)}, u32[]{:S(2)}, u32[]{:S(2)}) collective-permute-start(bf16[112,1152]{1,0:T(8,128)(2,1)S(1)} %slice.99), channel_id=1, source_target_pairs={{0,1},{1,2},{2,3},{3,0},{4,5},{5,6},{6,7},{7,4},{8,9},{9,10},{10,1... | collective-permute-start | bytes 774152 | tf_op jit(solution)/shard_map/ppermute | solution.py:39
  136.0 13.6 %collective-permute-start.3 = (bf16[112,1152]{1,0:T(8,128)(2,1)S(1)}, bf16[112,1152]{1,0:T(8,128)(2,1)S(1)}, u32[]{:S(2)}, u32[]{:S(2)}) collective-permute-start(bf16[112,1152]{1,0:T(8,128)(2,1)S(1)} %slice.100), channel_id=1, source_target_pairs={{0,3},{1,0},{2,1},{3,2},{4,7},{5,4},{6,5},{7,6},{8,11},{9,8},{10,9... | collective-permute-start | bytes 774152 | tf_op jit(solution)/shard_map/ppermute | solution.py:39
  144.2 11.0 %collective-permute-start.6 = (bf16[112,1152]{1,0:T(8,128)(2,1)S(1)}, bf16[112,1152]{1,0:T(8,128)(2,1)S(1)}, u32[]{:S(2)}, u32[]{:S(2)}) collective-permute-start(bf16[112,1152]{1,0:T(8,128)(2,1)S(1)} %slice.101), channel_id=1, source_target_pairs={{0,1},{1,2},{2,3},{3,0},{4,5},{5,6},{6,7},{7,4},{8,9},{9,10},{10,1... | collective-permute-start | bytes 774152 | tf_op jit(solution)/shard_map/ppermute | solution.py:39
  144.3 10.9 %collective-permute-start.7 = (bf16[112,1152]{1,0:T(8,128)(2,1)S(1)}, bf16[112,1152]{1,0:T(8,128)(2,1)S(1)}, u32[]{:S(2)}, u32[]{:S(2)}) collective-permute-start(bf16[112,1152]{1,0:T(8,128)(2,1)S(1)} %slice.102), channel_id=1, source_target_pairs={{0,3},{1,0},{2,1},{3,2},{4,7},{5,4},{6,5},{7,6},{8,11},{9,8},{10,9... | collective-permute-start | bytes 774152 | tf_op jit(solution)/shard_map/ppermute | solution.py:39
  155.3 2.0 copy-start.1
  155.3 15.1 %copy-start.4 = (f32[9216]{0:T(1024)S(1)}, f32[9216]{0:T(1024)}, u32[]{:S(2)}) copy-start(f32[9216]{0:T(1024)} %param.15) | copy-start | bytes 110596
  155.3 15.1 %copy-start.5 = (f32[768]{0:T(1024)S(1)}, f32[768]{0:T(1024)}, u32[]{:S(2)}) copy-start(f32[768]{0:T(1024)} %param.17) | copy-start | bytes 9220
  197.7 2.3 %copy-start.2 = (f32[2304]{0:T(1024)S(1)}, f32[2304]{0:T(1024)}, u32[]{:S(2)}) copy-start(f32[2304]{0:T(1024)} %param.19) | copy-start | bytes 27652
Sparse Core Ops, SparseCore 0:
  10.1 160.2 all-gather.2

commit v3 on v2

--- a/solution.py
+++ b/solution.py
@@ -48,6 +48,29 @@
     return block, below, above, jnp.concatenate([far_low, far_high], axis=0)
 
 
+def gather_rows(block, z_size, x_size, c_size):
+    x, c = lax.axis_index("x"), lax.axis_index("c")
+    rows, cols = block.shape
+    column = lax.all_gather(block, ("z", "c"), axis=0, tiled=True)
+    column = column.reshape(z_size, c_size * rows, cols)
+    part = z_size // c_size
+    mine = lax.dynamic_slice_in_dim(column, c * part, part, axis=0)
+    below = shift(mine, "x", x_size, 1)
+    above = shift(mine, "x", x_size, -1)
+    mid = part // 2
+    far = jnp.concatenate(
+        [shift(below[:mid], "x", x_size, 1), shift(above[mid:], "x", x_size, -1)], axis=0
+    )
+    full = jnp.zeros((z_size, x_size, c_size * rows, cols), block.dtype)
+    full = lax.dynamic_update_slice(full, column[:, None], (0, x, 0, 0))
+    for step, piece in ((-1, below), (1, above), (2, far)):
+        at = (x + step) % x_size
+        other = shift(piece, "c", c_size, 1)
+        full = lax.dynamic_update_slice(full, piece[:, None], (c * part, at, 0, 0))
+        full = lax.dynamic_update_slice(full, other[:, None], ((1 - c) * part, at, 0, 0))
+    return full.reshape(z_size * x_size * c_size * rows, cols)
+
+
 def per_device(sizes, rollouts, send_order, segment_ids, offsets, ln_gain,
                qkv_weight, qkv_scale, out_weight, out_scale):
     z_size, x_size, c_size, y_size = sizes
@@ -59,10 +82,8 @@
         for k in range(y_size):
             swap.append((z * y_size + k, (k * per_plane + b) * y_size + a))
     out_block = lax.ppermute(out_weight.T, ("z", "y"), swap)
-    qkv_cols = qkv_weight.shape[1]
-    both = jnp.concatenate([qkv_weight, out_block], axis=1)
-    both = lax.all_gather(both, DP, axis=0, tiled=True)
-    qkv_full, out_full = both[:, :qkv_cols], both[:, qkv_cols:]
+    qkv_full = gather_rows(qkv_weight, z_size, x_size, c_size)
+    out_full = lax.all_gather(out_block, DP, axis=0, tiled=True)
 
     response_count = send_order.shape[1]
     feature_count = rollouts.shape[1]
@@ -78,8 +99,8 @@
     half_count = feature_count // 2
     for half in range(2):
         slot_rows = rollouts[:, half * half_count : (half + 1) * half_count]
-        slot_rows = slot_rows.reshape(response_count, longest, half_count)
-        outgoing = jnp.take(slot_rows, send_order[0], axis=0)
+        slot_rows = slot_rows.reshape(response_count, longest // 2, 2, half_count)
+        outgoing = jnp.take(slot_rows, send_order[0], axis=0, mode="clip")
         arrived = lax.all_to_all(outgoing, DP, split_axis=0, concat_axis=0, tiled=True)
         part = arrived.reshape(response_count * longest, half_count)[take_rows]
         halves.append(part)
@@ -100,7 +121,11 @@
         queries = projected[:, member * head_size : (member + 1) * head_size]
         outputs.append(masked_attention(queries, key_rows, value_rows, segment))
     attended = jnp.concatenate(outputs, axis=1)
-    attended = lax.all_gather(attended, "y", axis=0, tiled=False)
+    everyone = jnp.zeros((y_size,) + attended.shape, attended.dtype)
+    for step in range(y_size):
+        piece = shift(attended, "y", y_size, step) if step else attended
+        everyone = lax.dynamic_update_slice(everyone, piece[None], ((y - step) % y_size, 0, 0))
+    attended = everyone
     out_full = out_full.reshape(y_size, feature_count, attended.shape[2])
     branch = 0.0
     for k in range(y_size):

time: 212 us -> 263 us (1.24)
  blocking collectives: 79 us -> 0 us
  waiting for transfers between devices: 59.9 us -> 124 us
  local copies, waits for them, and re-layouts: 11.7 us -> 49.3 us
  starting transfers between devices: 19.3 us -> 55.3 us
  matrix products: 21 us -> 17.3 us
  other arithmetic: 5.38 us -> 2.27 us
    all_to_all x1 -> x0, blocking collectives: 67.6 us -> none  [per_device(): lax.all_to_all(outgoing, DP, split_axis=0, concat_axis=0, tiled=True)]
    ppermute x8 -> x18, waiting for transfers between devices: 11.8 us -> 76.5 us  [shift(): lax.ppermute(value, axis, [(i, (i + step) % size) for i in range(size)])]
    all_to_all x1 -> x2, starting transfers between devices: 6.3 us -> 32.5 us  [per_device(): lax.all_to_all(outgoing, DP, split_axis=0, concat_axis=0, tiled=True)]
    dynamic_update_slice x0 -> x10, local copies, waits for them, and re-layouts: none -> 19.2 us  [the longest x3 8.58 us: gather_rows(): full = lax.dynamic_update_slice(full, piece[:, None], (c * part, at, 0, 0))]
    all_gather x1 -> x2, waiting for transfers between devices: 13.1 us -> 0.02 us  [the longest x1 0.02 us: per_device(): out_full = lax.all_gather(out_block, DP, axis=0, tiled=True)]
    all_to_all x1 -> x2, waiting for transfers between devices: 35 us -> 46.8 us  [per_device(): lax.all_to_all(outgoing, DP, split_axis=0, concat_axis=0, tiled=True)]
    all_gather x1 -> x0, blocking collectives: 11.5 us -> none  [per_device(): attended = lax.all_gather(attended, 'y', axis=0, tiled=False)]
    ppermute x8 -> x18, starting transfers between devices: 11.3 us -> 21.2 us  [shift(): lax.ppermute(value, axis, [(i, (i + step) % size) for i in range(size)])]
  transfers between devices with their start and end apart: 11 -> 23, of which waited for: 5 -> 11; matrix products, arithmetic and copies ran while one was open for 7% -> 23% of each run, Pallas kernels for 0% -> 0%
where the time goes in v3:
time: 263 us; the launch traced here: 262 us
  waiting for transfers between devices  124 us (47%)
  starting transfers between devices  55.3 us (21%)
  local copies, waits for them, and re-layouts  49.3 us (19%)
  matrix products  17.3 us (7%)
  between operations  14 us (5%)
    ppermute x18, waiting for transfers between devices, shift(): lax.ppermute(value, axis, [(i, (i + step) % size) for i in range(size)])  76.5 us
    all_to_all x2, waiting for transfers between devices, per_device(): lax.all_to_all(outgoing, DP, split_axis=0, concat_axis=0, tiled=True)  46.8 us
    all_to_all x2, starting transfers between devices, per_device(): lax.all_to_all(outgoing, DP, split_axis=0, concat_axis=0, tiled=True)  32.5 us
    ppermute x18, starting transfers between devices, shift(): lax.ppermute(value, axis, [(i, (i + step) % size) for i in range(size)])  21.2 us
    dot_general x1, matrix products, per_device(): projected = jnp.dot(normed, qkv_full, preferred_element_type=jnp.float32)  8.73 us
    dynamic_update_slice x3, local copies, waits for them, and re-layouts, gather_rows(): full = lax.dynamic_update_slice(full, piece[:, None], (c * part, at, 0, 0))  8.58 us
    dynamic_update_slice x3, local copies, waits for them, and re-layouts, gather_rows(): lax.dynamic_update_slice(full, other[:, None], ((1 - c) * part, at, 0, 0))  8.48 us
    dot_general x4, matrix products, per_device(): jnp.einsum('td,fd->tf', attended[k], out_full[k], preferred_element_type=...  7.4 us
  transfers between devices with their start and end apart: 23, of which 11 were waited for; matrix products, arithmetic and copies ran while one was open for 23% of the time, Pallas kernels for 0%

profile of v3, /device:TPU:1, one launch (start us, length us, event | category | flops | bytes accessed | tf_op | source)
XLA Modules:
  0.0 262.2 jit_solution(4829979572578123009)
XLA Ops:
  11.5 3.2 %gather_fusion = bf16[64,3,2,1152]{3,2,1,0:T(2,128)(2,1)} fusion(bf16[64,3,2,1152]{3,2,1,0:T(2,128)(2,1)S(1)} %reshape.112, s32[1024]{0:T(1024)S(1)} %get-tuple-element.12), kind=kCustom, calls=%fused_computation | custom fusion | bytes 1769728 | tf_op jit(solution)/shard_map/jit(_take)/gather | solution.py:103
  14.7 26.4 %all-to-all-start = ((bf16[64,3,2,1152]{3,2,1,0:T(2,128)(2,1)}), bf16[64,3,2,1152]{3,2,1,0:T(2,128)(2,1)S(1)}, u32[]{:S(2)}, u32[]{:S(2)}) async-start(bf16[64,3,2,1152]{3,2,1,0:T(2,128)(2,1)} %gather_fusion), calls=%async_computation | async-start | bytes 1769472 | tf_op jit(solution)/shard_map/all_to_all | solution.py:104
  41.5 3.3 %gather_fusion.3 = bf16[64,3,2,1152]{3,2,1,0:T(2,128)(2,1)} fusion(bf16[64,3,2,1152]{3,2,1,0:T(2,128)(2,1)S(1)} %reshape.114, s32[1024]{0:T(1024)S(1)} %get-tuple-element.12), kind=kCustom, calls=%fused_computation.3 | custom fusion | bytes 1769728 | tf_op jit(solution)/shard_map/jit(_take)/gather | solution.py:103
  44.8 25.7 %all-to-all-done = bf16[64,3,2,1152]{3,2,1,0:T(2,128)(2,1)S(1)} async-done(((bf16[64,3,2,1152]{3,2,1,0:T(2,128)(2,1)}), bf16[64,3,2,1152]{3,2,1,0:T(2,128)(2,1)S(1)}, u32[]{:S(2)}, u32[]{:S(2)}) %all-to-all-start) | async-done | bytes 884768 | tf_op jit(solution)/shard_map/all_to_all | solution.py:104
  70.5 6.1 %all-to-all-start.1 = ((bf16[64,3,2,1152]{3,2,1,0:T(2,128)(2,1)}), bf16[64,3,2,1152]{3,2,1,0:T(2,128)(2,1)S(1)}, u32[]{:S(2)}, u32[]{:S(2)}) async-start(bf16[64,3,2,1152]{3,2,1,0:T(2,128)(2,1)} %gather_fusion.3), calls=%async_computation.1 | async-start | bytes 1769472 | tf_op jit(solution)/shard_map/all_to_all | solution.py:104
  82.8 21.1 %all-to-all-done.1 = bf16[64,3,2,1152]{3,2,1,0:T(2,128)(2,1)S(1)} async-done(((bf16[64,3,2,1152]{3,2,1,0:T(2,128)(2,1)}), bf16[64,3,2,1152]{3,2,1,0:T(2,128)(2,1)S(1)}, u32[]{:S(2)}, u32[]{:S(2)}) %all-to-all-start.1) | async-done | bytes 884768 | tf_op jit(solution)/shard_map/all_to_all | solution.py:104
  114.4 5.1 %collective-permute-done.4 = bf16[224,1152]{1,0:T(8,128)(2,1)S(1)} collective-permute-done((bf16[224,1152]{1,0:T(8,128)(2,1)S(1)}, bf16[224,1152]{1,0:T(8,128)(2,1)S(1)}, u32[]{:S(2)}, u32[]{:S(2)}) %collective-permute-start.4) | collective-permute-done | bytes 516128 | tf_op jit(solution)/shard_map/ppermute | solution.py:39
  121.0 4.1 %collective-permute-done.2 = bf16[112,1152]{1,0:T(8,128)(2,1)S(1)} collective-permute-done((bf16[112,1152]{1,0:T(8,128)(2,1)S(1)}, bf16[112,1152]{1,0:T(8,128)(2,1)S(1)}, u32[]{:S(2)}, u32[]{:S(2)}) %collective-permute-start.2) | collective-permute-done | bytes 258080 | tf_op jit(solution)/shard_map/ppermute | solution.py:39
  126.6 3.9 %collective-permute-done.6 = bf16[112,1152]{1,0:T(8,128)(2,1)S(1)} collective-permute-done((bf16[112,1152]{1,0:T(8,128)(2,1)S(1)}, bf16[112,1152]{1,0:T(8,128)(2,1)S(1)}, u32[]{:S(2)}, u32[]{:S(2)}) %collective-permute-start.6) | collective-permute-done | bytes 258080 | tf_op jit(solution)/shard_map/ppermute | solution.py:39
  130.7 33.6 %collective-permute-done.8 = bf16[4,288,768]{2,1,0:T(8,128)(2,1)} collective-permute-done((bf16[4,288,768]{2,1,0:T(8,128)(2,1)S(1)}, bf16[4,288,768]{2,1,0:T(8,128)(2,1)}, u32[]{:S(2)}, u32[]{:S(2)}) %collective-permute-start.8) | collective-permute-done | bytes 1769504 | tf_op jit(solution)/shard_map/ppermute | solution.py:39
  168.5 6.1 %collective-permute-done.10 = bf16[4,288,768]{2,1,0:T(8,128)(2,1)} collective-permute-done((bf16[4,288,768]{2,1,0:T(8,128)(2,1)S(1)}, bf16[4,288,768]{2,1,0:T(8,128)(2,1)}, u32[]{:S(2)}, u32[]{:S(2)}) %collective-permute-start.10) | collective-permute-done | bytes 1769504 | tf_op jit(solution)/shard_map/ppermute | solution.py:39
  176.1 2.8 %collective-permute-start.11 = (bf16[4,288,768]{2,1,0:T(8,128)(2,1)}, bf16[4,288,768]{2,1,0:T(8,128)(2,1)}, u32[]{:S(2)}, u32[]{:S(2)}) collective-permute-start(bf16[4,288,768]{2,1,0:T(8,128)(2,1)} %collective-permute-done.10), channel_id=1, source_target_pairs={{0,4},{4,0},{1,5},{5,1},{2,6},{6,2},{3,7},{7,3},{8,12},{12,8},{9,1... | collective-permute-start | bytes 5308424 | tf_op jit(solution)/shard_map/ppermute | solution.py:39
  180.2 5.6 %collective-permute-done.12 = bf16[2,288,768]{2,1,0:T(8,128)(2,1)S(1)} collective-permute-done((bf16[2,288,768]{2,1,0:T(8,128)(2,1)S(1)}, bf16[2,288,768]{2,1,0:T(8,128)(2,1)S(1)}, u32[]{:S(2)}, u32[]{:S(2)}) %collective-permute-start.12) | collective-permute-done | bytes 884768 | tf_op jit(solution)/shard_map/ppermute | solution.py:39
  186.8 8.8 %collective-permute-done.13 = bf16[2,288,768]{2,1,0:T(8,128)(2,1)S(1)} collective-permute-done((bf16[2,288,768]{2,1,0:T(8,128)(2,1)S(1)}, bf16[2,288,768]{2,1,0:T(8,128)(2,1)S(1)}, u32[]{:S(2)}, u32[]{:S(2)}) %collective-permute-start.13) | collective-permute-done | bytes 884768 | tf_op jit(solution)/shard_map/ppermute | solution.py:39
  199.0 6.7 %broadcast_in_dim.68 = bf16[8,4,288,768]{3,2,1,0:T(8,128)(2,1)} broadcast(bf16[]{:T(256)} %constant.100.clone.1), dimensions={} | broadcast | bytes 14155778 | tf_op jit(solution)/shard_map/broadcast_in_dim | solution.py:64
  207.7 2.8 %bitcast_dynamic-update-slice_fusion.4 = bf16[8,4,288,768]{3,2,1,0:T(8,128)(2,1)} fusion(bf16[8,4,288,768]{3,2,1,0:T(8,128)(2,1)} %constant_dynamic-update-slice_fusion, s32[]{:T(128)S(6)} %select_n.156, s32[]{:T(128)S(6)} %select_n.158, bf16[4,288,768]{2,1,0:T(8,128)(2,1)} %collective-permute-done.8), kind=kLoop, calls=%fused_computation.33 | loop fusion | bytes 3538952 | tf_op jit(solution)/shard_map/dynamic_update_slice | solution.py:69
  210.5 2.9 %bitcast_dynamic-update-slice_fusion.3 = bf16[8,4,288,768]{3,2,1,0:T(8,128)(2,1)} fusion(bf16[8,4,288,768]{3,2,1,0:T(8,128)(2,1)} %bitcast_dynamic-update-slice_fusion.4, s32[]{:T(128)S(6)} %select_n.159, s32[]{:T(128)S(6)} %select_n.158, bf16[4,288,768]{2,1,0:T(8,128)(2,1)} %collective-permute-done.9), kind=kLoop, calls=%fused_computation.32 | loop fusion | bytes 3538952 | tf_op jit(solution)/shard_map/dynamic_update_slice | solution.py:70
  213.4 2.8 %bitcast_dynamic-update-slice_fusion.2 = bf16[8,4,288,768]{3,2,1,0:T(8,128)(2,1)} fusion(bf16[8,4,288,768]{3,2,1,0:T(8,128)(2,1)} %bitcast_dynamic-update-slice_fusion.3, s32[]{:T(128)S(6)} %select_n.156, s32[]{:T(128)S(6)} %select_n.161, bf16[4,288,768]{2,1,0:T(8,128)(2,1)} %collective-permute-done.10), kind=kLoop, calls=%fused_computation.31 | loop fusion | bytes 3538952 | tf_op jit(solution)/shard_map/dynamic_update_slice | solution.py:69
  219.0 2.9 %bitcast_dynamic-update-slice_fusion = bf16[8,4,288,768]{3,2,1,0:T(8,128)(2,1)} fusion(bf16[8,4,288,768]{3,2,1,0:T(8,128)(2,1)} %bitcast_dynamic-update-slice_fusion.1, s32[]{:T(128)S(6)} %select_n.156, s32[]{:T(128)S(6)} %select_n.163, bf16[4,288,768]{2,1,0:T(8,128)(2,1)} %constant_dynamic-update-slice_fusion.7), kind=kLoop, calls=%fused_computation.29 | loop fusion | bytes 3538952 | tf_op jit(solution)/shard_map/dynamic_update_slice | solution.py:69
  221.9 2.8 %bitcast_dynamic-update-slice_fusion.5 = bf16[8,4,288,768]{3,2,1,0:T(8,128)(2,1)} fusion(bf16[8,4,288,768]{3,2,1,0:T(8,128)(2,1)} %bitcast_dynamic-update-slice_fusion, s32[]{:T(128)S(6)} %select_n.159, s32[]{:T(128)S(6)} %select_n.163, bf16[4,288,768]{2,1,0:T(8,128)(2,1)} %collective-permute-done.14), kind=kLoop, calls=%fused_computation.34 | loop fusion | bytes 3538952 | tf_op jit(solution)/shard_map/dynamic_update_slice | solution.py:70
  224.8 8.7 %fusion.25 = bf16[224,768]{1,0:T(8,128)(2,1)S(1)} fusion(bf16[9216,768]{1,0:T(8,128)(2,1)} %bitcast.61, bf16[224,9216]{1,0:T(8,128)(2,1)S(1)} %copy-done.3, f32[9216]{0:T(1024)S(1)} %copy-done.14, f32[224]{0:T(256)S(1)} %add_rsqrt_fusion, f32[224]{0:T(256)S(1)} %broadcast_multiply_fusion, f32[768]{0:T(1024)S(1)} %copy-done.15), kind=kOutput, calls=%fused_computation.36 | convolution fusion | flops 3181559808 | bytes 18670336 | tf_op jit(solution)/shard_map/dot_general | solution.py:113
  235.0 3.5 %collective-permute-start.16 = (bf16[224,384]{0,1:T(8,128)(2,1)S(1)}, bf16[224,384]{0,1:T(8,128)(2,1)S(1)}, u32[]{:S(2)}, u32[]{:S(2)}) collective-permute-start(bf16[224,384]{0,1:T(8,128)(2,1)S(1)} %pad_maximum_fusion), channel_id=1, source_target_pairs={{0,2},{1,3},{2,0},{3,1},{4,6},{5,7},{6,4},{7,5},{8,10},{9,11},{10,... | collective-permute-start | bytes 516104 | tf_op jit(solution)/shard_map/ppermute | solution.py:39
  238.6 4.1 %collective-permute-done.15 = bf16[224,384]{0,1:T(8,128)(2,1)S(1)} collective-permute-done((bf16[224,384]{0,1:T(8,128)(2,1)S(1)}, bf16[224,384]{0,1:T(8,128)(2,1)S(1)}, u32[]{:S(2)}, u32[]{:S(2)}) %collective-permute-start.15) | collective-permute-done | bytes 172064 | tf_op jit(solution)/shard_map/ppermute | solution.py:39
  242.7 5.1 %collective-permute-done.16 = bf16[224,384]{0,1:T(8,128)(2,1)S(1)} collective-permute-done((bf16[224,384]{0,1:T(8,128)(2,1)S(1)}, bf16[224,384]{0,1:T(8,128)(2,1)S(1)}, u32[]{:S(2)}, u32[]{:S(2)}) %collective-permute-start.16) | collective-permute-done | bytes 172064 | tf_op jit(solution)/shard_map/ppermute | solution.py:39
  (117 shorter events, 49.9 us)
Async XLA Ops:
  6.5 70.1 %copy-start = (s32[1,64]{1,0:T(1,128)S(1)}, s32[1,64]{1,0:T(1,128)}, u32[]{:S(2)}) copy-start(s32[1,64]{1,0:T(1,128)} %param.12) | copy-start | bytes 772
  6.5 101.7 %all-gather.3.cloned.1.call-start = ((), (), s32[]{:S(2)}) async-start(), calls=%async_computation.2 | async-start | bytes 3760128 | tf_op jit(solution)/shard_map/all_gather | solution.py:54
  7.3 240.6 %all-gather.5.cloned.1.call-start = ((), (), s32[]{:S(2)}) async-start(), calls=%async_computation.3 | async-start | bytes 7188480 | tf_op jit(solution)/shard_map/all_gather | solution.py:86
  7.3 1.6 collective-permute-start.18
  14.7 55.8 %all-to-all-start = ((bf16[64,3,2,1152]{3,2,1,0:T(2,128)(2,1)}), bf16[64,3,2,1152]{3,2,1,0:T(2,128)(2,1)S(1)}, u32[]{:S(2)}, u32[]{:S(2)}) async-start(bf16[64,3,2,1152]{3,2,1,0:T(2,128)(2,1)} %gather_fusion), calls=%async_computation | async-start | bytes 1769472 | tf_op jit(solution)/shard_map/all_to_all | solution.py:104
  70.5 33.4 %all-to-all-start.1 = ((bf16[64,3,2,1152]{3,2,1,0:T(2,128)(2,1)}), bf16[64,3,2,1152]{3,2,1,0:T(2,128)(2,1)S(1)}, u32[]{:S(2)}, u32[]{:S(2)}) async-start(bf16[64,3,2,1152]{3,2,1,0:T(2,128)(2,1)} %gather_fusion.3), calls=%async_computation.1 | async-start | bytes 1769472 | tf_op jit(solution)/shard_map/all_to_all | solution.py:104
  80.1 31.4 %collective-permute-start = (bf16[224,1152]{1,0:T(8,128)(2,1)S(1)}, bf16[224,1152]{1,0:T(8,128)(2,1)S(1)}, u32[]{:S(2)}, u32[]{:S(2)}) collective-permute-start(bf16[224,1152]{1,0:T(8,128)(2,1)S(1)} %gather_fusion.2), channel_id=1, source_target_pairs={{0,1},{1,2},{2,3},{3,0},{4,5},{5,6},{6,7},{7,4},{8,9},{9,10},{10,1... | collective-permute-start | bytes 1548296 | tf_op jit(solution)/shard_map/ppermute | solution.py:39
  81.3 30.3 %collective-permute-start.1 = (bf16[224,1152]{1,0:T(8,128)(2,1)S(1)}, bf16[224,1152]{1,0:T(8,128)(2,1)S(1)}, u32[]{:S(2)}, u32[]{:S(2)}) collective-permute-start(bf16[224,1152]{1,0:T(8,128)(2,1)S(1)} %gather_fusion.2), channel_id=1, source_target_pairs={{0,3},{1,0},{2,1},{3,2},{4,7},{5,4},{6,5},{7,6},{8,11},{9,8},{10,9... | collective-permute-start | bytes 1548296 | tf_op jit(solution)/shard_map/ppermute | solution.py:39
  105.5 14.0 %collective-permute-start.4 = (bf16[224,1152]{1,0:T(8,128)(2,1)S(1)}, bf16[224,1152]{1,0:T(8,128)(2,1)S(1)}, u32[]{:S(2)}, u32[]{:S(2)}) collective-permute-start(bf16[224,1152]{1,0:T(8,128)(2,1)S(1)} %gather_fusion.4), channel_id=1, source_target_pairs={{0,1},{1,2},{2,3},{3,0},{4,5},{5,6},{6,7},{7,4},{8,9},{9,10},{10,1... | collective-permute-start | bytes 1548296 | tf_op jit(solution)/shard_map/ppermute | solution.py:39
  106.6 13.2 %collective-permute-start.5 = (bf16[224,1152]{1,0:T(8,128)(2,1)S(1)}, bf16[224,1152]{1,0:T(8,128)(2,1)}, u32[]{:S(2)}, u32[]{:S(2)}) collective-permute-start(bf16[224,1152]{1,0:T(8,128)(2,1)S(1)} %gather_fusion.4), channel_id=1, source_target_pairs={{0,3},{1,0},{2,1},{3,2},{4,7},{5,4},{6,5},{7,6},{8,11},{9,8},{10,9... | collective-permute-start | bytes 1548296 | tf_op jit(solution)/shard_map/ppermute | solution.py:39
  109.8 54.5 %collective-permute-start.8 = (bf16[4,288,768]{2,1,0:T(8,128)(2,1)S(1)}, bf16[4,288,768]{2,1,0:T(8,128)(2,1)}, u32[]{:S(2)}, u32[]{:S(2)}) collective-permute-start(bf16[4,288,768]{2,1,0:T(8,128)(2,1)S(1)} %constant_dynamic-slice_fusion), channel_id=1, source_target_pairs={{0,8},{8,16},{16,24},{24,0},{1,9},{9,17},{17,25},{25,1},{2,10},{10... | collective-permute-start | bytes 5308424 | tf_op jit(solution)/shard_map/ppermute | solution.py:39
  111.5 13.5 %collective-permute-start.2 = (bf16[112,1152]{1,0:T(8,128)(2,1)S(1)}, bf16[112,1152]{1,0:T(8,128)(2,1)S(1)}, u32[]{:S(2)}, u32[]{:S(2)}) collective-permute-start(bf16[112,1152]{1,0:T(8,128)(2,1)S(1)} %slice.94), channel_id=1, source_target_pairs={{0,1},{1,2},{2,3},{3,0},{4,5},{5,6},{6,7},{7,4},{8,9},{9,10},{10,1... | collective-permute-start | bytes 774152 | tf_op jit(solution)/shard_map/ppermute | solution.py:39
  111.7 13.6 %collective-permute-start.3 = (bf16[112,1152]{1,0:T(8,128)(2,1)S(1)}, bf16[112,1152]{1,0:T(8,128)(2,1)S(1)}, u32[]{:S(2)}, u32[]{:S(2)}) collective-permute-start(bf16[112,1152]{1,0:T(8,128)(2,1)S(1)} %slice.95), channel_id=1, source_target_pairs={{0,3},{1,0},{2,1},{3,2},{4,7},{5,4},{6,5},{7,6},{8,11},{9,8},{10,9... | collective-permute-start | bytes 774152 | tf_op jit(solution)/shard_map/ppermute | solution.py:39
  119.6 11.0 %collective-permute-start.6 = (bf16[112,1152]{1,0:T(8,128)(2,1)S(1)}, bf16[112,1152]{1,0:T(8,128)(2,1)S(1)}, u32[]{:S(2)}, u32[]{:S(2)}) collective-permute-start(bf16[112,1152]{1,0:T(8,128)(2,1)S(1)} %slice.96), channel_id=1, source_target_pairs={{0,1},{1,2},{2,3},{3,0},{4,5},{5,6},{6,7},{7,4},{8,9},{9,10},{10,1... | collective-permute-start | bytes 774152 | tf_op jit(solution)/shard_map/ppermute | solution.py:39
  120.7 53.9 %collective-permute-start.10 = (bf16[4,288,768]{2,1,0:T(8,128)(2,1)S(1)}, bf16[4,288,768]{2,1,0:T(8,128)(2,1)}, u32[]{:S(2)}, u32[]{:S(2)}) collective-permute-start(bf16[4,288,768]{2,1,0:T(8,128)(2,1)S(1)} %constant_dynamic-slice_fusion), channel_id=1, source_target_pairs={{0,24},{8,0},{16,8},{24,16},{1,25},{9,1},{17,9},{25,17},{2,26},{10... | collective-permute-start | bytes 5308424 | tf_op jit(solution)/shard_map/ppermute | solution.py:39
  125.1 5.6 %collective-permute-start.7 = (bf16[112,1152]{1,0:T(8,128)(2,1)S(1)}, bf16[112,1152]{1,0:T(8,128)(2,1)S(1)}, u32[]{:S(2)}, u32[]{:S(2)}) collective-permute-start(bf16[112,1152]{1,0:T(8,128)(2,1)S(1)} %slice.97), channel_id=1, source_target_pairs={{0,3},{1,0},{2,1},{3,2},{4,7},{5,4},{6,5},{7,6},{8,11},{9,8},{10,9... | collective-permute-start | bytes 774152 | tf_op jit(solution)/shard_map/ppermute | solution.py:39
  165.5 20.3 %collective-permute-start.12 = (bf16[2,288,768]{2,1,0:T(8,128)(2,1)S(1)}, bf16[2,288,768]{2,1,0:T(8,128)(2,1)S(1)}, u32[]{:S(2)}, u32[]{:S(2)}) collective-permute-start(bf16[2,288,768]{2,1,0:T(8,128)(2,1)S(1)} %slice.98), channel_id=1, source_target_pairs={{0,8},{8,16},{16,24},{24,0},{1,9},{9,17},{17,25},{25,1},{2,10},{10... | collective-permute-start | bytes 2654216 | tf_op jit(solution)/shard_map/ppermute | solution.py:39
  165.6 44.9 %collective-permute-start.9 = (bf16[4,288,768]{2,1,0:T(8,128)(2,1)}, bf16[4,288,768]{2,1,0:T(8,128)(2,1)}, u32[]{:S(2)}, u32[]{:S(2)}) collective-permute-start(bf16[4,288,768]{2,1,0:T(8,128)(2,1)} %collective-permute-done.8), channel_id=1, source_target_pairs={{0,4},{4,0},{1,5},{5,1},{2,6},{6,2},{3,7},{7,3},{8,12},{12,8},{9,1... | collective-permute-start | bytes 5308424 | tf_op jit(solution)/shard_map/ppermute | solution.py:39
  175.9 19.8 %collective-permute-start.13 = (bf16[2,288,768]{2,1,0:T(8,128)(2,1)S(1)}, bf16[2,288,768]{2,1,0:T(8,128)(2,1)S(1)}, u32[]{:S(2)}, u32[]{:S(2)}) collective-permute-start(bf16[2,288,768]{2,1,0:T(8,128)(2,1)S(1)} %slice.99), channel_id=1, source_target_pairs={{0,24},{8,0},{16,8},{24,16},{1,25},{9,1},{17,9},{25,17},{2,26},{10... | collective-permute-start | bytes 2654216 | tf_op jit(solution)/shard_map/ppermute | solution.py:39
  176.1 40.1 %collective-permute-start.11 = (bf16[4,288,768]{2,1,0:T(8,128)(2,1)}, bf16[4,288,768]{2,1,0:T(8,128)(2,1)}, u32[]{:S(2)}, u32[]{:S(2)}) collective-permute-start(bf16[4,288,768]{2,1,0:T(8,128)(2,1)} %collective-permute-done.10), channel_id=1, source_target_pairs={{0,4},{4,0},{1,5},{5,1},{2,6},{6,2},{3,7},{7,3},{8,12},{12,8},{9,1... | collective-permute-start | bytes 5308424 | tf_op jit(solution)/shard_map/ppermute | solution.py:39
  196.6 25.4 %collective-permute-start.14 = (bf16[4,288,768]{2,1,0:T(8,128)(2,1)}, bf16[4,288,768]{2,1,0:T(8,128)(2,1)}, u32[]{:S(2)}, u32[]{:S(2)}) collective-permute-start(bf16[4,288,768]{2,1,0:T(8,128)(2,1)} %constant_dynamic-update-slice_fusion.7), channel_id=1, source_target_pairs={{0,4},{4,0},{1,5},{5,1},{2,6},{6,2},{3,7},{7,3},{8,12},{12,8},{9,1... | collective-permute-start | bytes 5308424 | tf_op jit(solution)/shard_map/ppermute | solution.py:39
  234.9 7.8 %collective-permute-start.15 = (bf16[224,384]{0,1:T(8,128)(2,1)S(1)}, bf16[224,384]{0,1:T(8,128)(2,1)S(1)}, u32[]{:S(2)}, u32[]{:S(2)}) collective-permute-start(bf16[224,384]{0,1:T(8,128)(2,1)S(1)} %pad_maximum_fusion), channel_id=1, source_target_pairs={{0,1},{1,2},{2,3},{3,0},{4,5},{5,6},{6,7},{7,4},{8,9},{9,10},{10,1... | collective-permute-start | bytes 516104 | tf_op jit(solution)/shard_map/ppermute | solution.py:39
  235.0 12.8 %collective-permute-start.16 = (bf16[224,384]{0,1:T(8,128)(2,1)S(1)}, bf16[224,384]{0,1:T(8,128)(2,1)S(1)}, u32[]{:S(2)}, u32[]{:S(2)}) collective-permute-start(bf16[224,384]{0,1:T(8,128)(2,1)S(1)} %pad_maximum_fusion), channel_id=1, source_target_pairs={{0,2},{1,3},{2,0},{3,1},{4,6},{5,7},{6,4},{7,5},{8,10},{9,11},{10,... | collective-permute-start | bytes 516104 | tf_op jit(solution)/shard_map/ppermute | solution.py:39
  238.5 9.3 %collective-permute-start.17 = (bf16[224,384]{0,1:T(8,128)(2,1)S(1)}, bf16[224,384]{0,1:T(8,128)(2,1)S(1)}, u32[]{:S(2)}, u32[]{:S(2)}) collective-permute-start(bf16[224,384]{0,1:T(8,128)(2,1)S(1)} %pad_maximum_fusion), channel_id=1, source_target_pairs={{0,3},{1,0},{2,1},{3,2},{4,7},{5,4},{6,5},{7,6},{8,11},{9,8},{10,9... | collective-permute-start | bytes 516104 | tf_op jit(solution)/shard_map/ppermute | solution.py:39
  (15 other events, 152.3 us)
Sparse Core Ops, SparseCore 0:
  9.2 55.9 all-gather.2
  67.9 94.3 all-gather.4

commit v4 on v1

v4 whole, which is shorter than its diff:
```python
import functools

import jax
import jax.numpy as jnp
from jax import lax
from jax.experimental import pallas as pl
from jax.experimental.pallas import tpu as pltpu
from jax.sharding import Mesh, PartitionSpec as P

HEAD = 192
norm_epsilon = 1e-05
masked_score = -1e30
DP = ("z", "x", "c")


def shift(value, axis, size, step):
    return lax.ppermute(value, axis, [(i, (i + step) % size) for i in range(size)])


STEPS = (0, -1, 1, 2)


def normalize_kernel(y_size, pos_ref, *refs):
    pieces, gain_ref, out_ref = refs[:10], refs[10], refs[11]
    y = pos_ref[1]
    widths = (pieces[0].shape[1], pieces[5].shape[1])
    starts = (0, widths[0])
    mid = pieces[3].shape[0]
    block = 16
    total_count = y_size * sum(widths)
    owners = [lax.rem(y + step + y_size, y_size) for step in STEPS]
    gains = [
        gain_ref[owner, :, pl.ds(starts[half], widths[half])]
        for half in range(2)
        for owner in owners
    ]

    for side in range(2):
        def step(i, carry, side=side):
            near_rows = pl.ds(pl.multiple_of(side * mid + i * block, block), block)
            far_rows = pl.ds(pl.multiple_of(i * block, block), block)
            views = []
            for half in range(2):
                own, below, above, low, high = pieces[5 * half : 5 * half + 5]
                views += [(own, near_rows), (below, near_rows), (above, near_rows)]
                views += [((low, high)[side], far_rows)]
            total = 0.0
            for ref, rows in views:
                total = total + jnp.sum(ref[rows, :].astype(jnp.float32), axis=1, keepdims=True)
            mean = total / total_count
            total = 0.0
            for ref, rows in views:
                centered = ref[rows, :].astype(jnp.float32) - mean
                total = total + jnp.sum(centered * centered, axis=1, keepdims=True)
            rstd = lax.rsqrt(total / total_count + norm_epsilon)
            for at, (ref, rows) in enumerate(views):
                half, owner = at // 4, owners[at % 4]
                value = (ref[rows, :].astype(jnp.float32) - mean) * rstd * gains[at]
                out_ref[owner, near_rows, pl.ds(starts[half], widths[half])] = value.astype(
                    jnp.bfloat16
                )
            return carry

        lax.fori_loop(0, mid // block, step, 0)


def normalize(y_size, pos, pieces, gain):
    tokens = pieces[0].shape[0]
    columns = pieces[0].shape[1] + pieces[5].shape[1]
    vmem = pl.BlockSpec(memory_space=pltpu.VMEM)
    return pl.pallas_call(
        functools.partial(normalize_kernel, y_size),
        out_shape=jax.ShapeDtypeStruct((y_size, tokens, columns), jnp.bfloat16),
        in_specs=[pl.BlockSpec(memory_space=pltpu.SMEM)] + [vmem] * (len(pieces) + 1),
        out_specs=vmem,
        compiler_params=pltpu.CompilerParams(vmem_limit_bytes=24 * 2**20),
        cost_estimate=pl.CostEstimate(
            flops=20 * tokens * y_size * columns,
            bytes_accessed=8 * tokens * y_size * columns,
            transcendentals=tokens,
        ),
    )(pos, *pieces, gain)


def project_kernel(normed_ref, weight_ref, scale_ref, seg_col_ref, seg_row_ref, out_ref, weight, sems):
    chunks = sems.shape[0]
    y_size, _, features = normed_ref.shape
    per_owner = chunks // y_size
    depth = features // per_owner
    cols = weight.shape[1]
    copies = []
    for i in range(chunks):
        rows = pl.ds(i * depth, depth)
        copies.append(
            pltpu.make_async_copy(
                weight_ref.at[rows, pl.ds(0, cols)], weight.at[rows], sems.at[i]
            )
        )
    for copy in copies:
        copy.start()
    total = None
    for i in range(chunks):
        copies[i].wait()
        at = i % per_owner * depth
        term = jnp.dot(
            normed_ref[i // per_owner][:, at : at + depth],
            weight[i * depth : (i + 1) * depth],
            preferred_element_type=jnp.float32,
        )
        total = term if total is None else total + term
    projected = (total * scale_ref[...]).astype(jnp.bfloat16)
    tokens = projected.shape[0]
    allowed = seg_col_ref[...] == seg_row_ref[...]
    earlier = lax.broadcasted_iota(jnp.int32, (tokens, tokens), 1) <= lax.broadcasted_iota(
        jnp.int32, (tokens, tokens), 0
    )
    allowed = jnp.logical_and(allowed, earlier)
    heads = projected.shape[1] // HEAD - 2
    keys = projected[:, heads * HEAD : (heads + 1) * HEAD]
    values = projected[:, (heads + 1) * HEAD :]
    outs = []
    for head in range(heads):
        queries = projected[:, head * HEAD : (head + 1) * HEAD]
        scores = lax.dot_general(
            queries, keys, (((1,), (1,)), ((), ())), preferred_element_type=jnp.float32
        )
        scores = jnp.where(allowed, scores * float(HEAD) ** (-0.5), masked_score)
        peak = jnp.max(scores, axis=1, keepdims=True)
        exponent = jnp.exp(scores - peak)
        weights = (exponent / jnp.sum(exponent, axis=1, keepdims=True)).astype(jnp.bfloat16)
        outs.append(jnp.dot(weights, values, preferred_element_type=jnp.float32))
    out_ref[...] = jnp.concatenate(outs, axis=1).astype(jnp.bfloat16)


def project_and_attend(normed, weight, scale, segment):
    y_size, tokens, features = normed.shape
    cols = scale.shape[1]
    vmem = pl.BlockSpec(memory_space=pltpu.VMEM)
    return pl.pallas_call(
        project_kernel,
        out_shape=jax.ShapeDtypeStruct((tokens, cols - 2 * HEAD), jnp.bfloat16),
        in_specs=[vmem, pl.BlockSpec(memory_space=pl.ANY), vmem, vmem, vmem],
        out_specs=vmem,
        scratch_shapes=[
            pltpu.VMEM((y_size * features, cols), jnp.bfloat16),
            pltpu.SemaphoreType.DMA((2 * y_size,)),
        ],
        compiler_params=pltpu.CompilerParams(vmem_limit_bytes=56 * 2**20),
        cost_estimate=pl.CostEstimate(
            flops=2 * tokens * features * y_size * cols,
            bytes_accessed=2 * features * y_size * (cols + tokens),
            transcendentals=2 * tokens * tokens,
        ),
    )(normed, weight, scale, segment[:, None], segment[None, :])


def output_kernel(
    blocks, pos_ref, own, below, above, far, w0, w1, w2, w3, packed0, packed1, scale_ref, out_ref
):
    total = None
    for att, weight in ((own, w0), (below, w1), (above, w2), (far, w3)):
        term = lax.dot_general(
            att[...], weight[0], (((1,), (1,)), ((), ())), preferred_element_type=jnp.float32
        )
        total = term if total is None else total + term
    first = pl.program_id(0) < blocks
    packed = jnp.where(first, packed0[...], packed1[...]).astype(jnp.float32)
    out_ref[...] = (packed + total * scale_ref[...]).astype(jnp.bfloat16)


def project_out(pos, attended, weight, packed, scale):
    tokens, columns = packed[0].shape
    features = columns + packed[1].shape[1]
    y_size = weight.shape[0]
    depth = attended[0].shape[1]
    block = 384
    blocks = columns // block
    whole = pl.BlockSpec((tokens, depth), lambda n, p: (0, 0))

    def weight_spec(step):
        return pl.BlockSpec(
            (1, block, depth), lambda n, p: (lax.rem(p[1] + step + y_size, y_size), n, 0)
        )

    return pl.pallas_call(
        functools.partial(output_kernel, blocks),
        out_shape=jax.ShapeDtypeStruct((tokens, features), jnp.bfloat16),
        grid_spec=pltpu.PrefetchScalarGridSpec(
            num_scalar_prefetch=1,
            grid=(features // block,),
            in_specs=[whole] * 4
            + [weight_spec(step) for step in STEPS]
            + [
                pl.BlockSpec((tokens, block), lambda n, p: (0, jnp.minimum(n, blocks - 1))),
                pl.BlockSpec((tokens, block), lambda n, p: (0, jnp.maximum(n - blocks, 0))),
                pl.BlockSpec((1, block), lambda n, p: (0, n)),
            ],
            out_specs=pl.BlockSpec((tokens, block), lambda n, p: (0, n)),
        ),
        compiler_params=pltpu.CompilerParams(vmem_limit_bytes=24 * 2**20),
        cost_estimate=pl.CostEstimate(
            flops=2 * tokens * features * y_size * depth,
            bytes_accessed=2 * y_size * features * depth,
            transcendentals=0,
        ),
    )(pos, *attended, weight, weight, weight, weight, *packed, scale)


def per_device(sizes, rollouts, send_order, segment_ids, offsets, ln_gain,
               qkv_weight, qkv_scale, out_weight, out_scale):
    z_size, x_size, c_size, y_size = sizes
    x, y, c = lax.axis_index("x"), lax.axis_index("y"), lax.axis_index("c")
    pos = jnp.stack([x, y, c]).astype(jnp.int32)
    per_plane = z_size // y_size
    swap = []
    for z in range(z_size):
        a, b = z // per_plane, z % per_plane
        for k in range(y_size):
            swap.append((z * y_size + k, (k * per_plane + b) * y_size + a))
    out_block = lax.ppermute(out_weight.T, ("z", "y"), swap)
    response_count = send_order.shape[1]
    feature_count = rollouts.shape[1]
    longest = rollouts.shape[0] // response_count
    segment = segment_ids[0]
    token_count = segment.shape[0]
    within = jnp.clip(
        jnp.arange(token_count, dtype=jnp.int32) - offsets[0][segment], 0, longest - 1
    )
    take_rows = segment * longest + within
    first = feature_count * 2 // 3
    outgoing = []
    for start, width in ((0, first), (first, feature_count - first)):
        slot_rows = rollouts[:, start : start + width]
        slot_rows = slot_rows.reshape(response_count, longest // 2, 2, width)
        outgoing.append(jnp.take(slot_rows, send_order[0], axis=0, mode="clip"))
    qkv_cols = qkv_weight.shape[1]
    both = jnp.pad(qkv_weight, ((0, 0), (0, out_block.shape[1])))
    outgoing0, outgoing1, both, out_block = lax.optimization_barrier(
        (outgoing[0], outgoing[1], both, out_block)
    )
    both = lax.dynamic_update_slice(both, out_block, (0, qkv_cols))
    both = lax.all_gather(both, DP, axis=0, tiled=True)

    def exchange(block):
        arrived = lax.all_to_all(block, DP, split_axis=0, concat_axis=0, tiled=True)
        arrived = arrived.reshape(response_count * longest, block.shape[3])
        return jnp.take(arrived, take_rows, axis=0, mode="clip")

    mid = token_count // 2
    packed0 = exchange(outgoing0)
    below0, above0 = shift(packed0, "y", y_size, 1), shift(packed0, "y", y_size, -1)
    packed1 = exchange(outgoing1)
    below1, above1 = shift(packed1, "y", y_size, 1), shift(packed1, "y", y_size, -1)
    low0, high0 = shift(below0[:mid], "y", y_size, 1), shift(above0[mid:], "y", y_size, -1)
    low1, high1 = shift(below1[:mid], "y", y_size, 1), shift(above1[mid:], "y", y_size, -1)
    pieces = [packed0, below0, above0, low0, high0, packed1, below1, above1, low1, high1]
    normed = normalize(y_size, pos, pieces, ln_gain.reshape(y_size, 1, feature_count))
    attended = project_and_attend(normed, both, qkv_scale[None, :], segment)
    around = [attended] + [shift(attended, "y", y_size, step) for step in (1, -1, 2)]
    both, around[0] = lax.optimization_barrier((both, around[0]))
    weight = both[:, qkv_cols:].reshape(y_size, feature_count, attended.shape[1])
    return project_out(pos, around, weight, (packed0, packed1), out_scale[None, :])


def solution(mesh):
    chips = Mesh(mesh.devices.reshape(8, 4, 2, 4), ("z", "x", "c", "y"))
    in_specs = (
        P(DP, "y"),
        P(DP, None),
        P(DP, None),
        P(DP, None),
        P(),
        P(DP, "y"),
        P("y"),
        P("y", DP),
        P("y"),
    )

    def body(*args):
        return per_device((8, 4, 2, 4), *args)

    return jax.shard_map(
        body, mesh=chips, in_specs=in_specs, out_specs=P(DP, "y"), check_vma=False
    )
```

time: 232 us -> 189 us (0.81)
  waiting for transfers between devices: 137 us -> 45.6 us
  blocking collectives: 11.4 us -> 59 us
  Pallas kernels: 0 us -> 23 us
  matrix products: 18.4 us -> 0 us
  local copies, waits for them, and re-layouts: 12.4 us -> 25.4 us
  starting transfers between devices: 34 us -> 22.4 us
  other arithmetic: 5.7 us -> 0.11 us
    all_to_all x0 -> x1, blocking collectives: none -> 59 us  [exchange(): arrived = lax.all_to_all(block, DP, split_axis=0, concat_axis=0, tiled=True)]
    all_to_all x1, waiting for transfers between devices: 66.9 us -> 15.9 us  [exchange(): arrived = lax.all_to_all(block, DP, split_axis=0, concat_axis=0, tiled=True)]
    all_gather x2 -> x1, waiting for transfers between devices: 39.6 us -> 13.3 us  [per_device(): both = lax.all_gather(both, DP, axis=0, tiled=True)]
    pallas_call x0 -> x3, Pallas kernels: none -> 23 us  [the longest x1 11.6 us: project_and_attend(): pl.pallas_call(project_kernel, out_shape=jax.ShapeDtypeStruct((tokens, co...]
    all_to_all x1, starting transfers between devices: 26.6 us -> 7.38 us  [exchange(): arrived = lax.all_to_all(block, DP, split_axis=0, concat_axis=0, tiled=True)]
    dot_general x9 -> x0, matrix products: 18.4 us -> none  [the longest x1 9.9 us: per_device(): projected = jnp.dot(normed, qkv_full, preferred_element_type=jnp.float32)]
    ppermute x4 -> x11, waiting for transfers between devices: 29.3 us -> 16.3 us  [shift(): lax.ppermute(value, axis, [(i, (i + step) % size) for i in range(size)])]
    all_gather x1 -> x0, blocking collectives: 11.4 us -> none  [per_device(): attended = lax.all_gather(attended, 'y', axis=0, tiled=False)]
  transfers between devices with their start and end apart: 8 -> 14, of which waited for: 4 -> 6; matrix products, arithmetic and copies ran while one was open for 12% -> 12% of each run, Pallas kernels for 0% -> 3%
where the time goes in v4:
time: 189 us
  blocking collectives  59 us (31%)
  waiting for transfers between devices  45.6 us (24%)
  local copies, waits for them, and re-layouts  25.4 us (13%)
  Pallas kernels  23 us (12%)
  starting transfers between devices  22.4 us (12%)
  between operations  13.6 us (7%)
    all_to_all x1, blocking collectives, exchange(): arrived = lax.all_to_all(block, DP, split_axis=0, concat_axis=0, tiled=True)  59 us
    ppermute x11, waiting for transfers between devices, shift(): lax.ppermute(value, axis, [(i, (i + step) % size) for i in range(size)])  16.3 us
    all_to_all x1, waiting for transfers between devices, exchange(): arrived = lax.all_to_all(block, DP, split_axis=0, concat_axis=0, tiled=True)  15.9 us
    all_gather x1, waiting for transfers between devices, per_device(): both = lax.all_gather(both, DP, axis=0, tiled=True)  13.3 us
    ppermute x11, starting transfers between devices, shift(): lax.ppermute(value, axis, [(i, (i + step) % size) for i in range(size)])  13.3 us
    pallas_call x1, Pallas kernels, project_and_attend(): pl.pallas_call(project_kernel, out_shape=jax.ShapeDtypeStruct((tokens, co...  11.6 us
    all_to_all x1, starting transfers between devices, exchange(): arrived = lax.all_to_all(block, DP, split_axis=0, concat_axis=0, tiled=True)  7.38 us
    pallas_call x1, Pallas kernels, normalize(): pl.pallas_call(functools.partial(normalize_kernel, y_size), out_shape=jax...  6.07 us
  transfers between devices with their start and end apart: 14, of which 6 were waited for; matrix products, arithmetic and copies ran while one was open for 12% of the time, Pallas kernels for 3%

profile of v4, /device:TPU:1, one launch (start us, length us, event | category | flops | bytes accessed | tf_op | source)
XLA Modules:
  0.0 189.0 jit_solution(16587650981954382002)
XLA Ops:
  6.5 1.7 collective-permute-start
  10.3 3.0 %gather_fusion = bf16[64,3,2,1536]{3,2,1,0:T(2,128)(2,1)S(1)} fusion(bf16[64,3,2,1536]{3,2,1,0:T(2,128)(2,1)S(1)} %reshape.74, s32[1024]{0:T(1024)S(1)} %pad_clamp_fusion.2), kind=kCustom, calls=%fused_computation | custom fusion | bytes 2359552 | tf_op jit(solution)/shard_map/jit(_take)/gather | solution.py:235
  13.4 2.6 %gather_fusion.1 = bf16[64,3,2,768]{3,2,1,0:T(2,128)(2,1)} fusion(bf16[64,3,2,768]{3,2,1,0:T(2,128)(2,1)S(1)} %copy-done.4, s32[1024]{0:T(1024)S(1)} %pad_clamp_fusion.2), kind=kCustom, calls=%fused_computation.1 | custom fusion | bytes 1179904 | tf_op jit(solution)/shard_map/jit(_take)/gather | solution.py:235
  16.8 59.0 %all_to_all.10 = bf16[64,3,2,1536]{3,2,1,0:T(2,128)(2,1)S(1)} all-to-all(bf16[64,3,2,1536]{3,2,1,0:T(2,128)(2,1)S(1)} %gather_fusion), channel_id=1, replica_groups=mesh['z'=8,'x'=4,'c'=2,'y'=4] {'z','x','c'}, dimensions={0} | all-to-all | bytes 2359296 | tf_op jit(solution)/shard_map/all_to_all | solution.py:245
  75.8 7.4 %all-to-all-start.1 = ((bf16[64,3,2,768]{3,2,1,0:T(2,128)(2,1)}), bf16[64,3,2,768]{3,2,1,0:T(2,128)(2,1)}, u32[]{:S(2)}, u32[]{:S(2)}) async-start(bf16[64,3,2,768]{3,2,1,0:T(2,128)(2,1)} %gather_fusion.1), calls=%async_computation.1 | async-start | bytes 1179648 | tf_op jit(solution)/shard_map/all_to_all | solution.py:245
  83.2 1.9 gather_fusion.2
  85.6 1.2 gather_fusion.3
  87.1 2.4 %collective-permute-start.2 = (bf16[224,1536]{1,0:T(8,128)(2,1)S(1)}, bf16[224,1536]{1,0:T(8,128)(2,1)S(1)}, u32[]{:S(2)}, u32[]{:S(2)}) collective-permute-start(bf16[224,1536]{1,0:T(8,128)(2,1)S(1)} %gather_fusion.3), channel_id=1, source_target_pairs={{0,3},{1,0},{2,1},{3,2},{4,7},{5,4},{6,5},{7,6},{8,11},{9,8},{10,9... | collective-permute-start | bytes 2064392 | tf_op jit(solution)/shard_map/ppermute | solution.py:17
  89.5 15.9 %all-to-all-done.1 = bf16[64,3,2,768]{3,2,1,0:T(2,128)(2,1)} async-done(((bf16[64,3,2,768]{3,2,1,0:T(2,128)(2,1)}), bf16[64,3,2,768]{3,2,1,0:T(2,128)(2,1)}, u32[]{:S(2)}, u32[]{:S(2)}) %all-to-all-start.1) | async-done | bytes 589856 | tf_op jit(solution)/shard_map/all_to_all | solution.py:245
  105.4 2.0 %reshape.77 = bf16[384,768]{1,0:T(8,128)(2,1)S(1)} reshape(bf16[64,3,2,768]{3,2,1,0:T(2,128)(2,1)} %all-to-all-done.1) | data formatting | bytes 1179648 | tf_op jit(solution)/shard_map/reshape | solution.py:246
  108.8 2.5 %collective-permute-start.6 = (bf16[224,768]{1,0:T(8,128)(2,1)S(1)}, bf16[224,768]{1,0:T(8,128)(2,1)S(1)}, u32[]{:S(2)}, u32[]{:S(2)}) collective-permute-start(bf16[224,768]{1,0:T(8,128)(2,1)S(1)} %gather_fusion.4), channel_id=1, source_target_pairs={{0,3},{1,0},{2,1},{3,2},{4,7},{5,4},{6,5},{7,6},{8,11},{9,8},{10,9... | collective-permute-start | bytes 1032200 | tf_op jit(solution)/shard_map/ppermute | solution.py:17
  112.8 2.7 %collective-permute-start.4 = (bf16[112,1536]{1,0:T(8,128)(2,1)}, bf16[112,1536]{1,0:T(8,128)(2,1)}, u32[]{:S(2)}, u32[]{:S(2)}) collective-permute-start(bf16[112,1536]{1,0:T(8,128)(2,1)} %slice.39), channel_id=1, source_target_pairs={{0,3},{1,0},{2,1},{3,2},{4,7},{5,4},{6,5},{7,6},{8,11},{9,8},{10,9... | collective-permute-start | bytes 1032200 | tf_op jit(solution)/shard_map/ppermute | solution.py:17
  115.5 3.8 %collective-permute-done.5.refs_6_ = bf16[224,768]{1,0:T(8,128)(2,1)S(1)} collective-permute-done((bf16[224,768]{1,0:T(8,128)(2,1)S(1)}, bf16[224,768]{1,0:T(8,128)(2,1)S(1)}, u32[]{:S(2)}, u32[]{:S(2)}) %collective-permute-start.5) | collective-permute-done | bytes 344096 | tf_op jit(solution)/shard_map/ppermute | solution.py:17
  120.6 2.7 %collective-permute-start.8 = (bf16[112,768]{1,0:T(8,128)(2,1)}, bf16[112,768]{1,0:T(8,128)(2,1)}, u32[]{:S(2)}, u32[]{:S(2)}) collective-permute-start(bf16[112,768]{1,0:T(8,128)(2,1)} %slice.41), channel_id=1, source_target_pairs={{0,3},{1,0},{2,1},{3,2},{4,7},{5,4},{6,5},{7,6},{8,11},{9,8},{10,9... | collective-permute-start | bytes 516104 | tf_op jit(solution)/shard_map/ppermute | solution.py:17
  124.7 5.6 %collective-permute-done.7.refs_8_ = bf16[112,768]{1,0:T(8,128)(2,1)} collective-permute-done((bf16[112,768]{1,0:T(8,128)(2,1)}, bf16[112,768]{1,0:T(8,128)(2,1)}, u32[]{:S(2)}, u32[]{:S(2)}) %collective-permute-start.7) | collective-permute-done | bytes 172064 | tf_op jit(solution)/shard_map/ppermute | solution.py:17
  130.4 6.1 %shard_map.91.normed_ref = bf16[4,224,2304]{2,1,0:T(8,128)(2,1)S(1)} custom-call(s32[3]{0:T(128)S(1)} %pad_add_fusion.pos_ref, bf16[224,1536]{1,0:T(8,128)(2,1)S(1)} %gather_fusion.3, bf16[224,1536]{1,0:T(8,128)(2,1)S(1)} %collective-permute-done.1.refs_1_, bf16[224,1536]{1,0:T(8,128)(2,1)S(1)} %collective-permute-done.2.refs_2_, ...), custom_call_target="tpu_custom_call" | custom-call | flops 41287680 | bytes 16515072 | tf_op jit(solution)/shard_map/pallas_call | solution.py:71
  136.4 2.0 %copy-done.1 = bf16[4,224,2304]{2,1,0:T(8,128)(2,1)} copy-done((bf16[4,224,2304]{2,1,0:T(8,128)(2,1)}, bf16[4,224,2304]{2,1,0:T(8,128)(2,1)S(1)}, u32[]{:S(2)}) %copy-start.1) | copy-done | bytes 4128792
  138.5 13.3 %all-gather.2.cloned.1.call-done.weight_ref = bf16[9216,1152]{1,0:T(8,128)(2,1)} async-done(((bf16[144,1152]{1,0:T(8,128)(2,1)}), bf16[9216,1152]{1,0:T(8,128)(2,1)}) %all-gather.2.cloned.1.call-update) | async-done | bytes 21233680 | tf_op jit(solution)/shard_map/all_gather | solution.py:242
  151.8 11.6 %shard_map.92.own = bf16[224,384]{1,0:T(8,128)(2,1)} custom-call(bf16[4,224,2304]{2,1,0:T(8,128)(2,1)} %copy-done.1, bf16[9216,1152]{1,0:T(8,128)(2,1)} %all-gather.2.cloned.1.call-done.weight_ref, f32[1,768]{1,0:T(1,128)} %broadcast_in_dim.18.scale_ref, s32[224,1]{1,0:T(8,128)} %copy.10.seg_col_ref, s32[1,224]{1,0:T(1,128)} %seg_row_ref.1), custom_call_target="tpu_custom_call" | custom-call | flops 3170893824 | bytes 18284544 | tf_op jit(solution)/shard_map/pallas_call | solution.py:139
  163.3 1.8 collective-permute-start.10
  165.8 4.0 %slice.27 = bf16[9216,384]{1,0:T(8,128)(2,1)S(1)} slice(bf16[9216,1152]{1,0:T(8,128)(2,1)} %all-gather.2.cloned.1.call-done.weight_ref), slice={[0:9216], [768:1152]} | slice | bytes 14155776 | tf_op jit(solution)/shard_map/slice | solution.py:261
  169.8 2.5 %collective-permute-done.11.far = bf16[224,384]{1,0:T(8,128)(2,1)S(1)} collective-permute-done((bf16[224,384]{1,0:T(8,128)(2,1)}, bf16[224,384]{1,0:T(8,128)(2,1)S(1)}, u32[]{:S(2)}, u32[]{:S(2)}) %collective-permute-start.11) | collective-permute-done | bytes 172064 | tf_op jit(solution)/shard_map/ppermute | solution.py:17
  172.3 4.5 %collective-permute-done.9.below = bf16[224,384]{1,0:T(8,128)(2,1)S(1)} collective-permute-done((bf16[224,384]{1,0:T(8,128)(2,1)}, bf16[224,384]{1,0:T(8,128)(2,1)S(1)}, u32[]{:S(2)}, u32[]{:S(2)}) %collective-permute-start.9) | collective-permute-done | bytes 172064 | tf_op jit(solution)/shard_map/ppermute | solution.py:17
  176.8 5.3 %shard_map.93 = bf16[224,2304]{1,0:T(8,128)(2,1)} custom-call(s32[3]{0:T(128)S(1)} %pad_add_fusion.pos_ref, bf16[224,384]{1,0:T(8,128)(2,1)S(1)} %copy-done.2, bf16[224,384]{1,0:T(8,128)(2,1)S(1)} %collective-permute-done.9.below, bf16[224,384]{1,0:T(8,128)(2,1)S(1)} %collective-permute-done.10.above, bf16[224,384]{1,0:T(8,128)(2,1)S(1)} %collective-permute-done.11.far, ...), custom_call_target="tpu_custom_call" | custom-call | flops 1585446912 | bytes 7077888 | tf_op jit(solution)/shard_map/pallas_call | solution.py:185
  (60 shorter events, 10.2 us)
Async XLA Ops:
  6.5 76.7 %copy-start = (s32[1,64]{1,0:T(1,128)S(1)}, s32[1,64]{1,0:T(1,128)}, u32[]{:S(2)}) copy-start(s32[1,64]{1,0:T(1,128)} %param.12) | copy-start | bytes 772
  6.5 145.2 %all-gather.2.cloned.1.call-start = ((), (), s32[]{:S(2)}) async-start(), calls=%async_computation.2 | async-start | bytes 21565440 | tf_op jit(solution)/shard_map/all_gather | solution.py:242
  6.5 1.7 slice-start
  6.5 9.4 %collective-permute-start = (bf16[144,384]{1,0:T(8,128)(2,1)}, bf16[144,384]{1,0:T(8,128)(2,1)S(1)}, u32[]{:S(2)}, u32[]{:S(2)}) collective-permute-start(bf16[144,384]{1,0:T(8,128)(2,1)} %bitcast.25), channel_id=1, source_target_pairs={{0,0},{1,64},{2,128},{3,192},{32,32},{33,96},{34,160},{35,224},{64... | collective-permute-start | bytes 331784 | tf_op jit(solution)/shard_map/ppermute | solution.py:220
  10.3 3.0 %copy-start.4 = (bf16[64,3,2,768]{3,2,1,0:T(2,128)(2,1)S(1)}, bf16[64,3,2,768]{3,2,1,0:T(2,128)(2,1)}, u32[]{:S(2)}) copy-start(bf16[64,3,2,768]{3,2,1,0:T(2,128)(2,1)} %reshape.75) | copy-start | bytes 1769476
  13.4 2.6 %copy-start.6 = (bf16[144,768]{1,0:T(8,128)(2,1)S(1)}, bf16[144,768]{1,0:T(8,128)(2,1)}, u32[]{:S(2)}) copy-start(bf16[144,768]{1,0:T(8,128)(2,1)} %param.14) | copy-start | bytes 663556
  75.8 7.4 %copy-start.7 = (s32[1,224]{1,0:T(1,128)S(1)}, s32[1,224]{1,0:T(1,128)}, u32[]{:S(2)}) copy-start(s32[1,224]{1,0:T(1,128)} %seg_row_ref.1) | copy-start | bytes 2692
  75.8 29.7 %all-to-all-start.1 = ((bf16[64,3,2,768]{3,2,1,0:T(2,128)(2,1)}), bf16[64,3,2,768]{3,2,1,0:T(2,128)(2,1)}, u32[]{:S(2)}, u32[]{:S(2)}) async-start(bf16[64,3,2,768]{3,2,1,0:T(2,128)(2,1)} %gather_fusion.1), calls=%async_computation.1 | async-start | bytes 1179648 | tf_op jit(solution)/shard_map/all_to_all | solution.py:245
  86.8 24.5 %collective-permute-start.1 = (bf16[224,1536]{1,0:T(8,128)(2,1)S(1)}, bf16[224,1536]{1,0:T(8,128)(2,1)S(1)}, u32[]{:S(2)}, u32[]{:S(2)}) collective-permute-start(bf16[224,1536]{1,0:T(8,128)(2,1)S(1)} %gather_fusion.3), channel_id=1, source_target_pairs={{0,1},{1,2},{2,3},{3,0},{4,5},{5,6},{6,7},{7,4},{8,9},{9,10},{10,1... | collective-permute-start | bytes 2064392 | tf_op jit(solution)/shard_map/ppermute | solution.py:17
  87.1 25.0 %collective-permute-start.2 = (bf16[224,1536]{1,0:T(8,128)(2,1)S(1)}, bf16[224,1536]{1,0:T(8,128)(2,1)S(1)}, u32[]{:S(2)}, u32[]{:S(2)}) collective-permute-start(bf16[224,1536]{1,0:T(8,128)(2,1)S(1)} %gather_fusion.3), channel_id=1, source_target_pairs={{0,3},{1,0},{2,1},{3,2},{4,7},{5,4},{6,5},{7,6},{8,11},{9,8},{10,9... | collective-permute-start | bytes 2064392 | tf_op jit(solution)/shard_map/ppermute | solution.py:17
  108.5 15.5 %copy-start.9 = (f32[768]{0:T(1024)S(1)}, f32[768]{0:T(1024)}, u32[]{:S(2)}) copy-start(f32[768]{0:T(1024)} %param.15) | copy-start | bytes 9220
  108.5 21.8 %copy-start.3 = (f32[9216]{0:T(1024)S(1)}, f32[9216]{0:T(1024)}, u32[]{:S(2)}) copy-start(f32[9216]{0:T(1024)} %param.13) | copy-start | bytes 110596
  108.6 10.7 %collective-permute-start.5 = (bf16[224,768]{1,0:T(8,128)(2,1)S(1)}, bf16[224,768]{1,0:T(8,128)(2,1)S(1)}, u32[]{:S(2)}, u32[]{:S(2)}) collective-permute-start(bf16[224,768]{1,0:T(8,128)(2,1)S(1)} %gather_fusion.4), channel_id=1, source_target_pairs={{0,1},{1,2},{2,3},{3,0},{4,5},{5,6},{6,7},{7,4},{8,9},{9,10},{10,1... | collective-permute-start | bytes 1032200 | tf_op jit(solution)/shard_map/ppermute | solution.py:17
  108.8 11.1 %collective-permute-start.6 = (bf16[224,768]{1,0:T(8,128)(2,1)S(1)}, bf16[224,768]{1,0:T(8,128)(2,1)S(1)}, u32[]{:S(2)}, u32[]{:S(2)}) collective-permute-start(bf16[224,768]{1,0:T(8,128)(2,1)S(1)} %gather_fusion.4), channel_id=1, source_target_pairs={{0,3},{1,0},{2,1},{3,2},{4,7},{5,4},{6,5},{7,6},{8,11},{9,8},{10,9... | collective-permute-start | bytes 1032200 | tf_op jit(solution)/shard_map/ppermute | solution.py:17
  112.1 18.3 %collective-permute-start.3 = (bf16[112,1536]{1,0:T(8,128)(2,1)}, bf16[112,1536]{1,0:T(8,128)(2,1)S(1)}, u32[]{:S(2)}, u32[]{:S(2)}) collective-permute-start(bf16[112,1536]{1,0:T(8,128)(2,1)} %slice.38), channel_id=1, source_target_pairs={{0,1},{1,2},{2,3},{3,0},{4,5},{5,6},{6,7},{7,4},{8,9},{9,10},{10,1... | collective-permute-start | bytes 1032200 | tf_op jit(solution)/shard_map/ppermute | solution.py:17
  112.8 17.5 %collective-permute-start.4 = (bf16[112,1536]{1,0:T(8,128)(2,1)}, bf16[112,1536]{1,0:T(8,128)(2,1)}, u32[]{:S(2)}, u32[]{:S(2)}) collective-permute-start(bf16[112,1536]{1,0:T(8,128)(2,1)} %slice.39), channel_id=1, source_target_pairs={{0,3},{1,0},{2,1},{3,2},{4,7},{5,4},{6,5},{7,6},{8,11},{9,8},{10,9... | collective-permute-start | bytes 1032200 | tf_op jit(solution)/shard_map/ppermute | solution.py:17
  119.9 10.4 %collective-permute-start.7 = (bf16[112,768]{1,0:T(8,128)(2,1)}, bf16[112,768]{1,0:T(8,128)(2,1)}, u32[]{:S(2)}, u32[]{:S(2)}) collective-permute-start(bf16[112,768]{1,0:T(8,128)(2,1)} %slice.40), channel_id=1, source_target_pairs={{0,1},{1,2},{2,3},{3,0},{4,5},{5,6},{6,7},{7,4},{8,9},{9,10},{10,1... | collective-permute-start | bytes 516104 | tf_op jit(solution)/shard_map/ppermute | solution.py:17
  120.6 9.7 %collective-permute-start.8 = (bf16[112,768]{1,0:T(8,128)(2,1)}, bf16[112,768]{1,0:T(8,128)(2,1)}, u32[]{:S(2)}, u32[]{:S(2)}) collective-permute-start(bf16[112,768]{1,0:T(8,128)(2,1)} %slice.41), channel_id=1, source_target_pairs={{0,3},{1,0},{2,1},{3,2},{4,7},{5,4},{6,5},{7,6},{8,11},{9,8},{10,9... | collective-permute-start | bytes 516104 | tf_op jit(solution)/shard_map/ppermute | solution.py:17
  136.4 2.0 %copy-start.1 = (bf16[4,224,2304]{2,1,0:T(8,128)(2,1)}, bf16[4,224,2304]{2,1,0:T(8,128)(2,1)S(1)}, u32[]{:S(2)}) copy-start(bf16[4,224,2304]{2,1,0:T(8,128)(2,1)S(1)} %shard_map.91.normed_ref) | copy-start | bytes 12386308
  138.5 27.3 %copy-start.8 = (f32[2304]{0:T(1024)S(1)}, f32[2304]{0:T(1024)}, u32[]{:S(2)}) copy-start(f32[2304]{0:T(1024)} %param.17) | copy-start | bytes 27652
  163.3 6.5 %collective-permute-start.10 = (bf16[224,384]{1,0:T(8,128)(2,1)}, bf16[224,384]{1,0:T(8,128)(2,1)S(1)}, u32[]{:S(2)}, u32[]{:S(2)}) collective-permute-start(bf16[224,384]{1,0:T(8,128)(2,1)} %shard_map.92.own), channel_id=1, source_target_pairs={{0,3},{1,0},{2,1},{3,2},{4,7},{5,4},{6,5},{7,6},{8,11},{9,8},{10,9... | collective-permute-start | bytes 516104 | tf_op jit(solution)/shard_map/ppermute | solution.py:17
  165.1 7.2 %collective-permute-start.11 = (bf16[224,384]{1,0:T(8,128)(2,1)}, bf16[224,384]{1,0:T(8,128)(2,1)S(1)}, u32[]{:S(2)}, u32[]{:S(2)}) collective-permute-start(bf16[224,384]{1,0:T(8,128)(2,1)} %shard_map.92.own), channel_id=1, source_target_pairs={{0,2},{1,3},{2,0},{3,1},{4,6},{5,7},{6,4},{7,5},{8,10},{9,11},{10,... | collective-permute-start | bytes 516104 | tf_op jit(solution)/shard_map/ppermute | solution.py:17
  165.7 11.1 %collective-permute-start.9 = (bf16[224,384]{1,0:T(8,128)(2,1)}, bf16[224,384]{1,0:T(8,128)(2,1)S(1)}, u32[]{:S(2)}, u32[]{:S(2)}) collective-permute-start(bf16[224,384]{1,0:T(8,128)(2,1)} %shard_map.92.own), channel_id=1, source_target_pairs={{0,1},{1,2},{2,3},{3,0},{4,5},{5,6},{6,7},{7,4},{8,9},{9,10},{10,1... | collective-permute-start | bytes 516104 | tf_op jit(solution)/shard_map/ppermute | solution.py:17
  165.8 11.0 %copy-start.2 = (bf16[224,384]{1,0:T(8,128)(2,1)S(1)}, bf16[224,384]{1,0:T(8,128)(2,1)}, u32[]{:S(2)}) copy-start(bf16[224,384]{1,0:T(8,128)(2,1)} %shard_map.92.own) | copy-start | bytes 516100
  (3 other events, 2.9 us)
Sparse Core Ops, SparseCore 0:
  16.9 134.8 all-gather.1

commit v5 on v4

--- a/solution.py
+++ b/solution.py
@@ -154,43 +154,71 @@
     )(normed, weight, scale, segment[:, None], segment[None, :])
 
 
-def output_kernel(
-    blocks, pos_ref, own, below, above, far, w0, w1, w2, w3, packed0, packed1, scale_ref, out_ref
-):
+def near_kernel(pos_ref, own, below, above, w0, w1, w2, out_ref):
     total = None
-    for att, weight in ((own, w0), (below, w1), (above, w2), (far, w3)):
+    for att, weight in ((own, w0), (below, w1), (above, w2)):
         term = lax.dot_general(
             att[...], weight[0], (((1,), (1,)), ((), ())), preferred_element_type=jnp.float32
         )
         total = term if total is None else total + term
+    out_ref[...] = total
+
+
+def last_kernel(blocks, pos_ref, low, high, weight, near, packed0, packed1, scale_ref, out_ref):
+    far = jnp.concatenate([low[...], high[...]], axis=0)
+    total = near[...] + lax.dot_general(
+        far, weight[0], (((1,), (1,)), ((), ())), preferred_element_type=jnp.float32
+    )
     first = pl.program_id(0) < blocks
     packed = jnp.where(first, packed0[...], packed1[...]).astype(jnp.float32)
     out_ref[...] = (packed + total * scale_ref[...]).astype(jnp.bfloat16)
 
 
-def project_out(pos, attended, weight, packed, scale):
-    tokens, columns = packed[0].shape
-    features = columns + packed[1].shape[1]
-    y_size = weight.shape[0]
-    depth = attended[0].shape[1]
+def out_weight_spec(weight, block, step):
+    y_size, _, depth = weight.shape
+    return pl.BlockSpec(
+        (1, block, depth), lambda n, p: (lax.rem(p[1] + step + y_size, y_size), n, 0)
+    )
+
+
+def project_near(pos, attended, weight):
+    tokens, depth = attended[0].shape
+    features = weight.shape[1]
     block = 384
-    blocks = columns // block
-    whole = pl.BlockSpec((tokens, depth), lambda n, p: (0, 0))
-
-    def weight_spec(step):
-        return pl.BlockSpec(
-            (1, block, depth), lambda n, p: (lax.rem(p[1] + step + y_size, y_size), n, 0)
-        )
-
     return pl.pallas_call(
-        functools.partial(output_kernel, blocks),
+        near_kernel,
+        out_shape=jax.ShapeDtypeStruct((tokens, features), jnp.float32),
+        grid_spec=pltpu.PrefetchScalarGridSpec(
+            num_scalar_prefetch=1,
+            grid=(features // block,),
+            in_specs=[pl.BlockSpec((tokens, depth), lambda n, p: (0, 0))] * 3
+            + [out_weight_spec(weight, block, step) for step in STEPS[:3]],
+            out_specs=pl.BlockSpec((tokens, block), lambda n, p: (0, n)),
+        ),
+        compiler_params=pltpu.CompilerParams(vmem_limit_bytes=24 * 2**20),
+        cost_estimate=pl.CostEstimate(
+            flops=6 * tokens * features * depth, bytes_accessed=6 * features * depth, transcendentals=0
+        ),
+    )(pos, *attended, weight, weight, weight)
+
+
+def project_last(pos, low, high, near, weight, packed, scale):
+    tokens, features = near.shape
+    mid, depth = low.shape
+    block = 768
+    blocks = packed[0].shape[1] // block
+    rows = pl.BlockSpec((mid, depth), lambda n, p: (0, 0))
+    return pl.pallas_call(
+        functools.partial(last_kernel, blocks),
         out_shape=jax.ShapeDtypeStruct((tokens, features), jnp.bfloat16),
         grid_spec=pltpu.PrefetchScalarGridSpec(
             num_scalar_prefetch=1,
             grid=(features // block,),
-            in_specs=[whole] * 4
-            + [weight_spec(step) for step in STEPS]
-            + [
+            in_specs=[
+                rows,
+                rows,
+                out_weight_spec(weight, block, STEPS[3]),
+                pl.BlockSpec((tokens, block), lambda n, p: (0, n)),
                 pl.BlockSpec((tokens, block), lambda n, p: (0, jnp.minimum(n, blocks - 1))),
                 pl.BlockSpec((tokens, block), lambda n, p: (0, jnp.maximum(n - blocks, 0))),
                 pl.BlockSpec((1, block), lambda n, p: (0, n)),
@@ -199,11 +227,9 @@
         ),
         compiler_params=pltpu.CompilerParams(vmem_limit_bytes=24 * 2**20),
         cost_estimate=pl.CostEstimate(
-            flops=2 * tokens * features * y_size * depth,
-            bytes_accessed=2 * y_size * features * depth,
-            transcendentals=0,
-        ),
-    )(pos, *attended, weight, weight, weight, weight, *packed, scale)
+            flops=2 * tokens * features * depth, bytes_accessed=2 * features * depth, transcendentals=0
+        ),
+    )(pos, low, high, weight, near, *packed, scale)
 
 
 def per_device(sizes, rollouts, send_order, segment_ids, offsets, ln_gain,
@@ -256,10 +282,12 @@
     pieces = [packed0, below0, above0, low0, high0, packed1, below1, above1, low1, high1]
     normed = normalize(y_size, pos, pieces, ln_gain.reshape(y_size, 1, feature_count))
     attended = project_and_attend(normed, both, qkv_scale[None, :], segment)
-    around = [attended] + [shift(attended, "y", y_size, step) for step in (1, -1, 2)]
-    both, around[0] = lax.optimization_barrier((both, around[0]))
+    below, above = shift(attended, "y", y_size, 1), shift(attended, "y", y_size, -1)
+    low, high = shift(below[:mid], "y", y_size, 1), shift(above[mid:], "y", y_size, -1)
+    both, attended = lax.optimization_barrier((both, attended))
     weight = both[:, qkv_cols:].reshape(y_size, feature_count, attended.shape[1])
-    return project_out(pos, around, weight, (packed0, packed1), out_scale[None, :])
+    near = project_near(pos, (attended, below, above), weight)
+    return project_last(pos, low, high, near, weight, (packed0, packed1), out_scale[None, :])
 
 
 def solution(mesh):

time: 189 us -> 187 us (0.989)
  waiting for transfers between devices: 45.6 us -> 39 us
  starting transfers between devices: 22.4 us -> 25.5 us
    ppermute x11 -> x12, waiting for transfers between devices: 16.3 us -> 9.79 us  [shift(): lax.ppermute(value, axis, [(i, (i + step) % size) for i in range(size)])]
    ppermute x11 -> x12, starting transfers between devices: 13.3 us -> 16.4 us  [shift(): lax.ppermute(value, axis, [(i, (i + step) % size) for i in range(size)])]
    pallas_call x1 -> x2, Pallas kernels: 5.31 us -> 6.73 us  [the longest x1 3.75 us: project_near(): pl.pallas_call(near_kernel, out_shape=jax.ShapeDtypeStruct((tokens, featu...]
  transfers between devices with their start and end apart: 14 -> 15, of which waited for: 6 -> 5; matrix products, arithmetic and copies ran while one was open for 12% -> 12% of each run, Pallas kernels for 3% -> 5%
where the time goes in v5:
time: 187 us
  blocking collectives  59 us (32%)
  waiting for transfers between devices  39 us (21%)
  starting transfers between devices  25.5 us (14%)
  local copies, waits for them, and re-layouts  25.4 us (14%)
  Pallas kernels  24.4 us (13%)
  between operations  13.7 us (7%)
    all_to_all x1, blocking collectives, exchange(): arrived = lax.all_to_all(block, DP, split_axis=0, concat_axis=0, tiled=True)  59 us
    ppermute x12, starting transfers between devices, shift(): lax.ppermute(value, axis, [(i, (i + step) % size) for i in range(size)])  16.4 us
    all_to_all x1, waiting for transfers between devices, exchange(): arrived = lax.all_to_all(block, DP, split_axis=0, concat_axis=0, tiled=True)  15.9 us
    all_gather x1, waiting for transfers between devices, per_device(): both = lax.all_gather(both, DP, axis=0, tiled=True)  13.3 us
    pallas_call x1, Pallas kernels, project_and_attend(): pl.pallas_call(project_kernel, out_shape=jax.ShapeDtypeStruct((tokens, co...  11.6 us
    ppermute x12, waiting for transfers between devices, shift(): lax.ppermute(value, axis, [(i, (i + step) % size) for i in range(size)])  9.79 us
    all_to_all x1, starting transfers between devices, exchange(): arrived = lax.all_to_all(block, DP, split_axis=0, concat_axis=0, tiled=True)  7.38 us
    pallas_call x1, Pallas kernels, normalize(): pl.pallas_call(functools.partial(normalize_kernel, y_size), out_shape=jax...  6.07 us
  transfers between devices with their start and end apart: 15, of which 5 were waited for; matrix products, arithmetic and copies ran while one was open for 12% of the time, Pallas kernels for 5%

profile of v5, /device:TPU:1, one launch (start us, length us, event | category | flops | bytes accessed | tf_op | source)
XLA Modules:
  0.0 187.0 jit_solution(2235873644952642456)
XLA Ops:
  6.5 1.7 collective-permute-start
  10.3 3.0 %gather_fusion = bf16[64,3,2,1536]{3,2,1,0:T(2,128)(2,1)S(1)} fusion(bf16[64,3,2,1536]{3,2,1,0:T(2,128)(2,1)S(1)} %reshape.74, s32[1024]{0:T(1024)S(1)} %pad_clamp_fusion.2), kind=kCustom, calls=%fused_computation | custom fusion | bytes 2359552 | tf_op jit(solution)/shard_map/jit(_take)/gather | solution.py:261
  13.4 2.6 %gather_fusion.1 = bf16[64,3,2,768]{3,2,1,0:T(2,128)(2,1)} fusion(bf16[64,3,2,768]{3,2,1,0:T(2,128)(2,1)S(1)} %copy-done.4, s32[1024]{0:T(1024)S(1)} %pad_clamp_fusion.2), kind=kCustom, calls=%fused_computation.1 | custom fusion | bytes 1179904 | tf_op jit(solution)/shard_map/jit(_take)/gather | solution.py:261
  16.8 59.0 %all_to_all.10 = bf16[64,3,2,1536]{3,2,1,0:T(2,128)(2,1)S(1)} all-to-all(bf16[64,3,2,1536]{3,2,1,0:T(2,128)(2,1)S(1)} %gather_fusion), channel_id=1, replica_groups=mesh['z'=8,'x'=4,'c'=2,'y'=4] {'z','x','c'}, dimensions={0} | all-to-all | bytes 2359296 | tf_op jit(solution)/shard_map/all_to_all | solution.py:271
  75.8 7.4 %all-to-all-start.1 = ((bf16[64,3,2,768]{3,2,1,0:T(2,128)(2,1)}), bf16[64,3,2,768]{3,2,1,0:T(2,128)(2,1)}, u32[]{:S(2)}, u32[]{:S(2)}) async-start(bf16[64,3,2,768]{3,2,1,0:T(2,128)(2,1)} %gather_fusion.1), calls=%async_computation.1 | async-start | bytes 1179648 | tf_op jit(solution)/shard_map/all_to_all | solution.py:271
  83.2 1.9 gather_fusion.2
  85.6 1.2 gather_fusion.3
  87.1 2.4 %collective-permute-start.2 = (bf16[224,1536]{1,0:T(8,128)(2,1)S(1)}, bf16[224,1536]{1,0:T(8,128)(2,1)S(1)}, u32[]{:S(2)}, u32[]{:S(2)}) collective-permute-start(bf16[224,1536]{1,0:T(8,128)(2,1)S(1)} %gather_fusion.3), channel_id=1, source_target_pairs={{0,3},{1,0},{2,1},{3,2},{4,7},{5,4},{6,5},{7,6},{8,11},{9,8},{10,9... | collective-permute-start | bytes 2064392 | tf_op jit(solution)/shard_map/ppermute | solution.py:17
  89.5 15.9 %all-to-all-done.1 = bf16[64,3,2,768]{3,2,1,0:T(2,128)(2,1)} async-done(((bf16[64,3,2,768]{3,2,1,0:T(2,128)(2,1)}), bf16[64,3,2,768]{3,2,1,0:T(2,128)(2,1)}, u32[]{:S(2)}, u32[]{:S(2)}) %all-to-all-start.1) | async-done | bytes 589856 | tf_op jit(solution)/shard_map/all_to_all | solution.py:271
  105.4 2.0 %reshape.77 = bf16[384,768]{1,0:T(8,128)(2,1)S(1)} reshape(bf16[64,3,2,768]{3,2,1,0:T(2,128)(2,1)} %all-to-all-done.1) | data formatting | bytes 1179648 | tf_op jit(solution)/shard_map/reshape | solution.py:272
  108.8 2.5 %collective-permute-start.6 = (bf16[224,768]{1,0:T(8,128)(2,1)S(1)}, bf16[224,768]{1,0:T(8,128)(2,1)S(1)}, u32[]{:S(2)}, u32[]{:S(2)}) collective-permute-start(bf16[224,768]{1,0:T(8,128)(2,1)S(1)} %gather_fusion.4), channel_id=1, source_target_pairs={{0,3},{1,0},{2,1},{3,2},{4,7},{5,4},{6,5},{7,6},{8,11},{9,8},{10,9... | collective-permute-start | bytes 1032200 | tf_op jit(solution)/shard_map/ppermute | solution.py:17
  112.8 2.7 %collective-permute-start.4 = (bf16[112,1536]{1,0:T(8,128)(2,1)}, bf16[112,1536]{1,0:T(8,128)(2,1)}, u32[]{:S(2)}, u32[]{:S(2)}) collective-permute-start(bf16[112,1536]{1,0:T(8,128)(2,1)} %slice.47), channel_id=1, source_target_pairs={{0,3},{1,0},{2,1},{3,2},{4,7},{5,4},{6,5},{7,6},{8,11},{9,8},{10,9... | collective-permute-start | bytes 1032200 | tf_op jit(solution)/shard_map/ppermute | solution.py:17
  115.5 3.8 %collective-permute-done.5.refs_6_ = bf16[224,768]{1,0:T(8,128)(2,1)S(1)} collective-permute-done((bf16[224,768]{1,0:T(8,128)(2,1)S(1)}, bf16[224,768]{1,0:T(8,128)(2,1)S(1)}, u32[]{:S(2)}, u32[]{:S(2)}) %collective-permute-start.5) | collective-permute-done | bytes 344096 | tf_op jit(solution)/shard_map/ppermute | solution.py:17
  120.6 2.7 %collective-permute-start.8 = (bf16[112,768]{1,0:T(8,128)(2,1)}, bf16[112,768]{1,0:T(8,128)(2,1)}, u32[]{:S(2)}, u32[]{:S(2)}) collective-permute-start(bf16[112,768]{1,0:T(8,128)(2,1)} %slice.49), channel_id=1, source_target_pairs={{0,3},{1,0},{2,1},{3,2},{4,7},{5,4},{6,5},{7,6},{8,11},{9,8},{10,9... | collective-permute-start | bytes 516104 | tf_op jit(solution)/shard_map/ppermute | solution.py:17
  124.8 5.6 %collective-permute-done.7.refs_8_ = bf16[112,768]{1,0:T(8,128)(2,1)} collective-permute-done((bf16[112,768]{1,0:T(8,128)(2,1)}, bf16[112,768]{1,0:T(8,128)(2,1)}, u32[]{:S(2)}, u32[]{:S(2)}) %collective-permute-start.7) | collective-permute-done | bytes 172064 | tf_op jit(solution)/shard_map/ppermute | solution.py:17
  130.3 6.1 %shard_map.91.normed_ref = bf16[4,224,2304]{2,1,0:T(8,128)(2,1)S(1)} custom-call(s32[3]{0:T(128)S(1)} %pad_add_fusion.pos_ref, bf16[224,1536]{1,0:T(8,128)(2,1)S(1)} %gather_fusion.3, bf16[224,1536]{1,0:T(8,128)(2,1)S(1)} %collective-permute-done.1.refs_1_, bf16[224,1536]{1,0:T(8,128)(2,1)S(1)} %collective-permute-done.2.refs_2_, ...), custom_call_target="tpu_custom_call" | custom-call | flops 41287680 | bytes 16515072 | tf_op jit(solution)/shard_map/pallas_call | solution.py:71
  136.4 2.0 %copy-done.1 = bf16[4,224,2304]{2,1,0:T(8,128)(2,1)} copy-done((bf16[4,224,2304]{2,1,0:T(8,128)(2,1)}, bf16[4,224,2304]{2,1,0:T(8,128)(2,1)S(1)}, u32[]{:S(2)}) %copy-start.1) | copy-done | bytes 4128792
  138.4 13.3 %all-gather.2.cloned.1.call-done.weight_ref = bf16[9216,1152]{1,0:T(8,128)(2,1)} async-done(((bf16[144,1152]{1,0:T(8,128)(2,1)}), bf16[9216,1152]{1,0:T(8,128)(2,1)}) %all-gather.2.cloned.1.call-update) | async-done | bytes 21233680 | tf_op jit(solution)/shard_map/all_gather | solution.py:268
  151.8 11.6 %shard_map.92.own = bf16[224,384]{1,0:T(8,128)(2,1)} custom-call(bf16[4,224,2304]{2,1,0:T(8,128)(2,1)} %copy-done.1, bf16[9216,1152]{1,0:T(8,128)(2,1)} %all-gather.2.cloned.1.call-done.weight_ref, f32[1,768]{1,0:T(1,128)} %broadcast_in_dim.18.scale_ref, s32[224,1]{1,0:T(8,128)} %copy.10.seg_col_ref, s32[1,224]{1,0:T(1,128)} %seg_row_ref.1), custom_call_target="tpu_custom_call" | custom-call | flops 3170893824 | bytes 18284544 | tf_op jit(solution)/shard_map/pallas_call | solution.py:139
  163.9 2.2 %collective-permute-start.11 = (bf16[224,384]{1,0:T(8,128)(2,1)}, bf16[224,384]{1,0:T(8,128)(2,1)S(1)}, u32[]{:S(2)}, u32[]{:S(2)}) collective-permute-start(bf16[224,384]{1,0:T(8,128)(2,1)} %shard_map.92.own), channel_id=1, source_target_pairs={{0,3},{1,0},{2,1},{3,2},{4,7},{5,4},{6,5},{7,6},{8,11},{9,8},{10,9... | collective-permute-start | bytes 516104 | tf_op jit(solution)/shard_map/ppermute | solution.py:17
  166.1 4.0 %slice.35 = bf16[9216,384]{1,0:T(8,128)(2,1)S(1)} slice(bf16[9216,1152]{1,0:T(8,128)(2,1)} %all-gather.2.cloned.1.call-done.weight_ref), slice={[0:9216], [768:1152]} | slice | bytes 14155776 | tf_op jit(solution)/shard_map/slice | solution.py:288
  170.7 2.7 %collective-permute-start.12 = (bf16[112,384]{1,0:T(8,128)(2,1)S(1)}, bf16[112,384]{1,0:T(8,128)(2,1)S(1)}, u32[]{:S(2)}, u32[]{:S(2)}) collective-permute-start(bf16[112,384]{1,0:T(8,128)(2,1)S(1)} %slice.51), channel_id=1, source_target_pairs={{0,3},{1,0},{2,1},{3,2},{4,7},{5,4},{6,5},{7,6},{8,11},{9,8},{10,9... | collective-permute-start | bytes 258056 | tf_op jit(solution)/shard_map/ppermute | solution.py:17
  173.4 3.7 %shard_map.93.near = f32[224,2304]{1,0:T(8,128)S(1)} custom-call(s32[3]{0:T(128)S(1)} %pad_add_fusion.pos_ref, bf16[224,384]{1,0:T(8,128)(2,1)S(1)} %copy-done.2, bf16[224,384]{1,0:T(8,128)(2,1)S(1)} %collective-permute-done.9.below, bf16[224,384]{1,0:T(8,128)(2,1)S(1)} %collective-permute-done.11.above, bf16[4,2304,384]{2,1,0:T(8,128)(2,1)S(1)} %bitcast.15, ...), custom_call_target="tpu_custom_call" | custom-call | flops 1189085184 | bytes 5308416 | tf_op jit(solution)/shard_map/pallas_call | solution.py:188
  177.2 3.0 %shard_map.94 = bf16[224,2304]{1,0:T(8,128)(2,1)} custom-call(s32[3]{0:T(128)S(1)} %pad_add_fusion.pos_ref, bf16[112,384]{1,0:T(8,128)(2,1)S(1)} %collective-permute-done.10.low, bf16[112,384]{1,0:T(8,128)(2,1)S(1)} %collective-permute-done.12.high, bf16[4,2304,384]{2,1,0:T(8,128)(2,1)S(1)} %bitcast.18, f32[224,2304]{1,0:T(8,128)S(1)} %shard_map.93.near, ...), custom_call_target="tpu_custom_call" | custom-call | flops 396361728 | bytes 1769472 | tf_op jit(solution)/shard_map/pallas_call | solution.py:211
  (65 shorter events, 10.7 us)
Async XLA Ops:
  6.5 76.6 %copy-start = (s32[1,64]{1,0:T(1,128)S(1)}, s32[1,64]{1,0:T(1,128)}, u32[]{:S(2)}) copy-start(s32[1,64]{1,0:T(1,128)} %param.12) | copy-start | bytes 772
  6.5 145.2 %all-gather.2.cloned.1.call-start = ((), (), s32[]{:S(2)}) async-start(), calls=%async_computation.2 | async-start | bytes 21565440 | tf_op jit(solution)/shard_map/all_gather | solution.py:268
  6.5 9.4 %collective-permute-start = (bf16[144,384]{1,0:T(8,128)(2,1)}, bf16[144,384]{1,0:T(8,128)(2,1)S(1)}, u32[]{:S(2)}, u32[]{:S(2)}) collective-permute-start(bf16[144,384]{1,0:T(8,128)(2,1)} %bitcast.25), channel_id=1, source_target_pairs={{0,0},{1,64},{2,128},{3,192},{32,32},{33,96},{34,160},{35,224},{64... | collective-permute-start | bytes 331784 | tf_op jit(solution)/shard_map/ppermute | solution.py:246
  10.3 3.0 %copy-start.4 = (bf16[64,3,2,768]{3,2,1,0:T(2,128)(2,1)S(1)}, bf16[64,3,2,768]{3,2,1,0:T(2,128)(2,1)}, u32[]{:S(2)}) copy-start(bf16[64,3,2,768]{3,2,1,0:T(2,128)(2,1)} %reshape.75) | copy-start | bytes 1769476
  13.4 2.6 %copy-start.6 = (bf16[144,768]{1,0:T(8,128)(2,1)S(1)}, bf16[144,768]{1,0:T(8,128)(2,1)}, u32[]{:S(2)}) copy-start(bf16[144,768]{1,0:T(8,128)(2,1)} %param.14) | copy-start | bytes 663556
  75.8 7.4 %copy-start.7 = (s32[1,224]{1,0:T(1,128)S(1)}, s32[1,224]{1,0:T(1,128)}, u32[]{:S(2)}) copy-start(s32[1,224]{1,0:T(1,128)} %seg_row_ref.1) | copy-start | bytes 2692
  75.8 29.7 %all-to-all-start.1 = ((bf16[64,3,2,768]{3,2,1,0:T(2,128)(2,1)}), bf16[64,3,2,768]{3,2,1,0:T(2,128)(2,1)}, u32[]{:S(2)}, u32[]{:S(2)}) async-start(bf16[64,3,2,768]{3,2,1,0:T(2,128)(2,1)} %gather_fusion.1), calls=%async_computation.1 | async-start | bytes 1179648 | tf_op jit(solution)/shard_map/all_to_all | solution.py:271
  86.8 24.5 %collective-permute-start.1 = (bf16[224,1536]{1,0:T(8,128)(2,1)S(1)}, bf16[224,1536]{1,0:T(8,128)(2,1)S(1)}, u32[]{:S(2)}, u32[]{:S(2)}) collective-permute-start(bf16[224,1536]{1,0:T(8,128)(2,1)S(1)} %gather_fusion.3), channel_id=1, source_target_pairs={{0,1},{1,2},{2,3},{3,0},{4,5},{5,6},{6,7},{7,4},{8,9},{9,10},{10,1... | collective-permute-start | bytes 2064392 | tf_op jit(solution)/shard_map/ppermute | solution.py:17
  87.1 25.0 %collective-permute-start.2 = (bf16[224,1536]{1,0:T(8,128)(2,1)S(1)}, bf16[224,1536]{1,0:T(8,128)(2,1)S(1)}, u32[]{:S(2)}, u32[]{:S(2)}) collective-permute-start(bf16[224,1536]{1,0:T(8,128)(2,1)S(1)} %gather_fusion.3), channel_id=1, source_target_pairs={{0,3},{1,0},{2,1},{3,2},{4,7},{5,4},{6,5},{7,6},{8,11},{9,8},{10,9... | collective-permute-start | bytes 2064392 | tf_op jit(solution)/shard_map/ppermute | solution.py:17
  108.5 15.6 %copy-start.9 = (f32[768]{0:T(1024)S(1)}, f32[768]{0:T(1024)}, u32[]{:S(2)}) copy-start(f32[768]{0:T(1024)} %param.15) | copy-start | bytes 9220
  108.5 21.8 %copy-start.3 = (f32[9216]{0:T(1024)S(1)}, f32[9216]{0:T(1024)}, u32[]{:S(2)}) copy-start(f32[9216]{0:T(1024)} %param.13) | copy-start | bytes 110596
  108.5 10.7 %collective-permute-start.5 = (bf16[224,768]{1,0:T(8,128)(2,1)S(1)}, bf16[224,768]{1,0:T(8,128)(2,1)S(1)}, u32[]{:S(2)}, u32[]{:S(2)}) collective-permute-start(bf16[224,768]{1,0:T(8,128)(2,1)S(1)} %gather_fusion.4), channel_id=1, source_target_pairs={{0,1},{1,2},{2,3},{3,0},{4,5},{5,6},{6,7},{7,4},{8,9},{9,10},{10,1... | collective-permute-start | bytes 1032200 | tf_op jit(solution)/shard_map/ppermute | solution.py:17
  108.8 11.1 %collective-permute-start.6 = (bf16[224,768]{1,0:T(8,128)(2,1)S(1)}, bf16[224,768]{1,0:T(8,128)(2,1)S(1)}, u32[]{:S(2)}, u32[]{:S(2)}) collective-permute-start(bf16[224,768]{1,0:T(8,128)(2,1)S(1)} %gather_fusion.4), channel_id=1, source_target_pairs={{0,3},{1,0},{2,1},{3,2},{4,7},{5,4},{6,5},{7,6},{8,11},{9,8},{10,9... | collective-permute-start | bytes 1032200 | tf_op jit(solution)/shard_map/ppermute | solution.py:17
  112.1 18.3 %collective-permute-start.3 = (bf16[112,1536]{1,0:T(8,128)(2,1)}, bf16[112,1536]{1,0:T(8,128)(2,1)S(1)}, u32[]{:S(2)}, u32[]{:S(2)}) collective-permute-start(bf16[112,1536]{1,0:T(8,128)(2,1)} %slice.46), channel_id=1, source_target_pairs={{0,1},{1,2},{2,3},{3,0},{4,5},{5,6},{6,7},{7,4},{8,9},{9,10},{10,1... | collective-permute-start | bytes 1032200 | tf_op jit(solution)/shard_map/ppermute | solution.py:17
  112.8 17.5 %collective-permute-start.4 = (bf16[112,1536]{1,0:T(8,128)(2,1)}, bf16[112,1536]{1,0:T(8,128)(2,1)}, u32[]{:S(2)}, u32[]{:S(2)}) collective-permute-start(bf16[112,1536]{1,0:T(8,128)(2,1)} %slice.47), channel_id=1, source_target_pairs={{0,3},{1,0},{2,1},{3,2},{4,7},{5,4},{6,5},{7,6},{8,11},{9,8},{10,9... | collective-permute-start | bytes 1032200 | tf_op jit(solution)/shard_map/ppermute | solution.py:17
  120.0 10.4 %collective-permute-start.7 = (bf16[112,768]{1,0:T(8,128)(2,1)}, bf16[112,768]{1,0:T(8,128)(2,1)}, u32[]{:S(2)}, u32[]{:S(2)}) collective-permute-start(bf16[112,768]{1,0:T(8,128)(2,1)} %slice.48), channel_id=1, source_target_pairs={{0,1},{1,2},{2,3},{3,0},{4,5},{5,6},{6,7},{7,4},{8,9},{9,10},{10,1... | collective-permute-start | bytes 516104 | tf_op jit(solution)/shard_map/ppermute | solution.py:17
  120.6 9.7 %collective-permute-start.8 = (bf16[112,768]{1,0:T(8,128)(2,1)}, bf16[112,768]{1,0:T(8,128)(2,1)}, u32[]{:S(2)}, u32[]{:S(2)}) collective-permute-start(bf16[112,768]{1,0:T(8,128)(2,1)} %slice.49), channel_id=1, source_target_pairs={{0,3},{1,0},{2,1},{3,2},{4,7},{5,4},{6,5},{7,6},{8,11},{9,8},{10,9... | collective-permute-start | bytes 516104 | tf_op jit(solution)/shard_map/ppermute | solution.py:17
  136.4 2.0 %copy-start.1 = (bf16[4,224,2304]{2,1,0:T(8,128)(2,1)}, bf16[4,224,2304]{2,1,0:T(8,128)(2,1)S(1)}, u32[]{:S(2)}) copy-start(bf16[4,224,2304]{2,1,0:T(8,128)(2,1)S(1)} %shard_map.91.normed_ref) | copy-start | bytes 12386308
  138.4 27.7 %copy-start.8 = (f32[2304]{0:T(1024)S(1)}, f32[2304]{0:T(1024)}, u32[]{:S(2)}) copy-start(f32[2304]{0:T(1024)} %param.17) | copy-start | bytes 27652
  163.3 7.2 %collective-permute-start.9 = (bf16[224,384]{1,0:T(8,128)(2,1)}, bf16[224,384]{1,0:T(8,128)(2,1)S(1)}, u32[]{:S(2)}, u32[]{:S(2)}) collective-permute-start(bf16[224,384]{1,0:T(8,128)(2,1)} %shard_map.92.own), channel_id=1, source_target_pairs={{0,1},{1,2},{2,3},{3,0},{4,5},{5,6},{6,7},{7,4},{8,9},{9,10},{10,1... | collective-permute-start | bytes 516104 | tf_op jit(solution)/shard_map/ppermute | solution.py:17
  163.9 6.7 %collective-permute-start.11 = (bf16[224,384]{1,0:T(8,128)(2,1)}, bf16[224,384]{1,0:T(8,128)(2,1)S(1)}, u32[]{:S(2)}, u32[]{:S(2)}) collective-permute-start(bf16[224,384]{1,0:T(8,128)(2,1)} %shard_map.92.own), channel_id=1, source_target_pairs={{0,3},{1,0},{2,1},{3,2},{4,7},{5,4},{6,5},{7,6},{8,11},{9,8},{10,9... | collective-permute-start | bytes 516104 | tf_op jit(solution)/shard_map/ppermute | solution.py:17
  166.1 7.3 %copy-start.2 = (bf16[224,384]{1,0:T(8,128)(2,1)S(1)}, bf16[224,384]{1,0:T(8,128)(2,1)}, u32[]{:S(2)}) copy-start(bf16[224,384]{1,0:T(8,128)(2,1)} %shard_map.92.own) | copy-start | bytes 516100
  170.6 6.6 %collective-permute-start.10 = (bf16[112,384]{1,0:T(8,128)(2,1)S(1)}, bf16[112,384]{1,0:T(8,128)(2,1)S(1)}, u32[]{:S(2)}, u32[]{:S(2)}) collective-permute-start(bf16[112,384]{1,0:T(8,128)(2,1)S(1)} %slice.50), channel_id=1, source_target_pairs={{0,1},{1,2},{2,3},{3,0},{4,5},{5,6},{6,7},{7,4},{8,9},{9,10},{10,1... | collective-permute-start | bytes 258056 | tf_op jit(solution)/shard_map/ppermute | solution.py:17
  170.7 6.5 %collective-permute-start.12 = (bf16[112,384]{1,0:T(8,128)(2,1)S(1)}, bf16[112,384]{1,0:T(8,128)(2,1)S(1)}, u32[]{:S(2)}, u32[]{:S(2)}) collective-permute-start(bf16[112,384]{1,0:T(8,128)(2,1)S(1)} %slice.51), channel_id=1, source_target_pairs={{0,3},{1,0},{2,1},{3,2},{4,7},{5,4},{6,5},{7,6},{8,11},{9,8},{10,9... | collective-permute-start | bytes 258056 | tf_op jit(solution)/shard_map/ppermute | solution.py:17
  (4 other events, 4.5 us)
Sparse Core Ops, SparseCore 0:
  16.9 134.8 all-gather.1

commit v6 on v4

--- a/solution.py
+++ b/solution.py
@@ -154,56 +154,61 @@
     )(normed, weight, scale, segment[:, None], segment[None, :])
 
 
-def output_kernel(
-    blocks, pos_ref, own, below, above, far, w0, w1, w2, w3, packed0, packed1, scale_ref, out_ref
-):
+def near_kernel(pos_ref, own, below, above, weight, out_ref):
+    y_size = weight.shape[0]
     total = None
-    for att, weight in ((own, w0), (below, w1), (above, w2), (far, w3)):
+    for att, step in zip((own, below, above), STEPS):
         term = lax.dot_general(
-            att[...], weight[0], (((1,), (1,)), ((), ())), preferred_element_type=jnp.float32
+            att[...],
+            weight[lax.rem(pos_ref[1] + step + y_size, y_size)],
+            (((1,), (1,)), ((), ())),
+            preferred_element_type=jnp.float32,
         )
         total = term if total is None else total + term
-    first = pl.program_id(0) < blocks
-    packed = jnp.where(first, packed0[...], packed1[...]).astype(jnp.float32)
-    out_ref[...] = (packed + total * scale_ref[...]).astype(jnp.bfloat16)
-
-
-def project_out(pos, attended, weight, packed, scale):
-    tokens, columns = packed[0].shape
-    features = columns + packed[1].shape[1]
+    out_ref[...] = total
+
+
+def last_kernel(pos_ref, low, high, weight, near, packed0, packed1, scale_ref, out_ref):
     y_size = weight.shape[0]
-    depth = attended[0].shape[1]
-    block = 384
-    blocks = columns // block
-    whole = pl.BlockSpec((tokens, depth), lambda n, p: (0, 0))
-
-    def weight_spec(step):
-        return pl.BlockSpec(
-            (1, block, depth), lambda n, p: (lax.rem(p[1] + step + y_size, y_size), n, 0)
-        )
-
+    far = jnp.concatenate([low[...], high[...]], axis=0)
+    start = 0
+    for packed in (packed0, packed1):
+        at = slice(start, start + packed.shape[1])
+        start += packed.shape[1]
+        total = near[:, at] + lax.dot_general(
+            far,
+            weight[lax.rem(pos_ref[1] + STEPS[3], y_size), at],
+            (((1,), (1,)), ((), ())),
+            preferred_element_type=jnp.float32,
+        )
+        value = packed[...].astype(jnp.float32) + total * scale_ref[:, at]
+        out_ref[:, at] = value.astype(jnp.bfloat16)
+
+
+def on_vmem(kernel, out_shape, flops, pos, *operands):
+    vmem = pl.BlockSpec(memory_space=pltpu.VMEM)
     return pl.pallas_call(
-        functools.partial(output_kernel, blocks),
-        out_shape=jax.ShapeDtypeStruct((tokens, features), jnp.bfloat16),
-        grid_spec=pltpu.PrefetchScalarGridSpec(
-            num_scalar_prefetch=1,
-            grid=(features // block,),
-            in_specs=[whole] * 4
-            + [weight_spec(step) for step in STEPS]
-            + [
-                pl.BlockSpec((tokens, block), lambda n, p: (0, jnp.minimum(n, blocks - 1))),
-                pl.BlockSpec((tokens, block), lambda n, p: (0, jnp.maximum(n - blocks, 0))),
-                pl.BlockSpec((1, block), lambda n, p: (0, n)),
-            ],
-            out_specs=pl.BlockSpec((tokens, block), lambda n, p: (0, n)),
-        ),
+        kernel,
+        out_shape=out_shape,
+        in_specs=[pl.BlockSpec(memory_space=pltpu.SMEM)] + [vmem] * len(operands),
+        out_specs=vmem,
         compiler_params=pltpu.CompilerParams(vmem_limit_bytes=24 * 2**20),
-        cost_estimate=pl.CostEstimate(
-            flops=2 * tokens * features * y_size * depth,
-            bytes_accessed=2 * y_size * features * depth,
-            transcendentals=0,
-        ),
-    )(pos, *attended, weight, weight, weight, weight, *packed, scale)
+        cost_estimate=pl.CostEstimate(flops=flops, bytes_accessed=8 * 2**20, transcendentals=0),
+    )(pos, *operands)
+
+
+def project_near(pos, attended, weight):
+    tokens, depth = attended[0].shape
+    features = weight.shape[1]
+    shape = jax.ShapeDtypeStruct((tokens, features), jnp.float32)
+    return on_vmem(near_kernel, shape, 6 * tokens * features * depth, pos, *attended, weight)
+
+
+def project_last(pos, low, high, near, weight, packed, scale):
+    tokens, features = near.shape
+    shape = jax.ShapeDtypeStruct((tokens, features), jnp.bfloat16)
+    flops = 2 * tokens * features * low.shape[1]
+    return on_vmem(last_kernel, shape, flops, pos, low, high, weight, near, *packed, scale)
 
 
 def per_device(sizes, rollouts, send_order, segment_ids, offsets, ln_gain,
@@ -256,10 +261,12 @@
     pieces = [packed0, below0, above0, low0, high0, packed1, below1, above1, low1, high1]
     normed = normalize(y_size, pos, pieces, ln_gain.reshape(y_size, 1, feature_count))
     attended = project_and_attend(normed, both, qkv_scale[None, :], segment)
-    around = [attended] + [shift(attended, "y", y_size, step) for step in (1, -1, 2)]
-    both, around[0] = lax.optimization_barrier((both, around[0]))
+    below, above = shift(attended, "y", y_size, 1), shift(attended, "y", y_size, -1)
+    low, high = shift(below[:mid], "y", y_size, 1), shift(above[mid:], "y", y_size, -1)
+    both, attended = lax.optimization_barrier((both, attended))
     weight = both[:, qkv_cols:].reshape(y_size, feature_count, attended.shape[1])
-    return project_out(pos, around, weight, (packed0, packed1), out_scale[None, :])
+    near = project_near(pos, (attended, below, above), weight)
+    return project_last(pos, low, high, near, weight, (packed0, packed1), out_scale[None, :])
 
 
 def solution(mesh):

time: 189 us -> 186 us (0.984)
  waiting for transfers between devices: 45.6 us -> 39 us
  starting transfers between devices: 22.4 us -> 25.5 us
    ppermute x11 -> x12, waiting for transfers between devices: 16.3 us -> 9.79 us  [shift(): lax.ppermute(value, axis, [(i, (i + step) % size) for i in range(size)])]
    ppermute x11 -> x12, starting transfers between devices: 13.3 us -> 16.4 us  [shift(): lax.ppermute(value, axis, [(i, (i + step) % size) for i in range(size)])]
    pallas_call x1 -> x2, Pallas kernels: 5.31 us -> 4.75 us  [on_vmem(): pl.pallas_call(kernel, out_shape=out_shape, in_specs=[pl.BlockSpec(memory...]
  transfers between devices with their start and end apart: 14 -> 15, of which waited for: 6 -> 5; matrix products, arithmetic and copies ran while one was open for 12% -> 12% of each run, Pallas kernels for 3% -> 5%
where the time goes in v6:
time: 186 us; the launch traced here: 185 us
  blocking collectives  59 us (32%)
  waiting for transfers between devices  39 us (21%)
  starting transfers between devices  25.5 us (14%)
  local copies, waits for them, and re-layouts  25.4 us (14%)
  Pallas kernels  22.4 us (12%)
  between operations  13.7 us (7%)
    all_to_all x1, blocking collectives, exchange(): arrived = lax.all_to_all(block, DP, split_axis=0, concat_axis=0, tiled=True)  59 us
    ppermute x12, starting transfers between devices, shift(): lax.ppermute(value, axis, [(i, (i + step) % size) for i in range(size)])  16.4 us
    all_to_all x1, waiting for transfers between devices, exchange(): arrived = lax.all_to_all(block, DP, split_axis=0, concat_axis=0, tiled=True)  15.9 us
    all_gather x1, waiting for transfers between devices, per_device(): both = lax.all_gather(both, DP, axis=0, tiled=True)  13.3 us
    pallas_call x1, Pallas kernels, project_and_attend(): pl.pallas_call(project_kernel, out_shape=jax.ShapeDtypeStruct((tokens, co...  11.6 us
    ppermute x12, waiting for transfers between devices, shift(): lax.ppermute(value, axis, [(i, (i + step) % size) for i in range(size)])  9.79 us
    all_to_all x1, starting transfers between devices, exchange(): arrived = lax.all_to_all(block, DP, split_axis=0, concat_axis=0, tiled=True)  7.38 us
    pallas_call x1, Pallas kernels, normalize(): pl.pallas_call(functools.partial(normalize_kernel, y_size), out_shape=jax...  6.07 us
  transfers between devices with their start and end apart: 15, of which 5 were waited for; matrix products, arithmetic and copies ran while one was open for 12% of the time, Pallas kernels for 5%

profile of v6, /device:TPU:1, one launch (start us, length us, event | category | flops | bytes accessed | tf_op | source)
XLA Modules:
  0.0 185.0 jit_solution(2420997625380471151)
XLA Ops:
  6.5 1.7 collective-permute-start
  10.3 3.0 %gather_fusion = bf16[64,3,2,1536]{3,2,1,0:T(2,128)(2,1)S(1)} fusion(bf16[64,3,2,1536]{3,2,1,0:T(2,128)(2,1)S(1)} %reshape.74, s32[1024]{0:T(1024)S(1)} %pad_clamp_fusion.2), kind=kCustom, calls=%fused_computation | custom fusion | bytes 2359552 | tf_op jit(solution)/shard_map/jit(_take)/gather | solution.py:240
  13.4 2.6 %gather_fusion.1 = bf16[64,3,2,768]{3,2,1,0:T(2,128)(2,1)} fusion(bf16[64,3,2,768]{3,2,1,0:T(2,128)(2,1)S(1)} %copy-done.4, s32[1024]{0:T(1024)S(1)} %pad_clamp_fusion.2), kind=kCustom, calls=%fused_computation.1 | custom fusion | bytes 1179904 | tf_op jit(solution)/shard_map/jit(_take)/gather | solution.py:240
  16.8 59.0 %all_to_all.10 = bf16[64,3,2,1536]{3,2,1,0:T(2,128)(2,1)S(1)} all-to-all(bf16[64,3,2,1536]{3,2,1,0:T(2,128)(2,1)S(1)} %gather_fusion), channel_id=1, replica_groups=mesh['z'=8,'x'=4,'c'=2,'y'=4] {'z','x','c'}, dimensions={0} | all-to-all | bytes 2359296 | tf_op jit(solution)/shard_map/all_to_all | solution.py:250
  75.8 7.4 %all-to-all-start.1 = ((bf16[64,3,2,768]{3,2,1,0:T(2,128)(2,1)}), bf16[64,3,2,768]{3,2,1,0:T(2,128)(2,1)}, u32[]{:S(2)}, u32[]{:S(2)}) async-start(bf16[64,3,2,768]{3,2,1,0:T(2,128)(2,1)} %gather_fusion.1), calls=%async_computation.1 | async-start | bytes 1179648 | tf_op jit(solution)/shard_map/all_to_all | solution.py:250
  83.2 1.9 %gather_fusion.2 = s32[224]{0:T(256)S(1)} fusion(s32[64]{0:T(128)S(1)} %bitcast.14, s32[1024]{0:T(1024)S(1)} %pad_clamp_fusion.1), kind=kCustom, calls=%fused_computation.2 | custom fusion | bytes 2688 | tf_op jit(solution)/shard_map/gather | solution.py:232
  85.6 1.2 gather_fusion.3
  87.1 2.4 %collective-permute-start.2 = (bf16[224,1536]{1,0:T(8,128)(2,1)S(1)}, bf16[224,1536]{1,0:T(8,128)(2,1)S(1)}, u32[]{:S(2)}, u32[]{:S(2)}) collective-permute-start(bf16[224,1536]{1,0:T(8,128)(2,1)S(1)} %gather_fusion.3), channel_id=1, source_target_pairs={{0,3},{1,0},{2,1},{3,2},{4,7},{5,4},{6,5},{7,6},{8,11},{9,8},{10,9... | collective-permute-start | bytes 2064392 | tf_op jit(solution)/shard_map/ppermute | solution.py:17
  89.5 15.9 %all-to-all-done.1 = bf16[64,3,2,768]{3,2,1,0:T(2,128)(2,1)} async-done(((bf16[64,3,2,768]{3,2,1,0:T(2,128)(2,1)}), bf16[64,3,2,768]{3,2,1,0:T(2,128)(2,1)}, u32[]{:S(2)}, u32[]{:S(2)}) %all-to-all-start.1) | async-done | bytes 589856 | tf_op jit(solution)/shard_map/all_to_all | solution.py:250
  105.4 2.0 %reshape.77 = bf16[384,768]{1,0:T(8,128)(2,1)S(1)} reshape(bf16[64,3,2,768]{3,2,1,0:T(2,128)(2,1)} %all-to-all-done.1) | data formatting | bytes 1179648 | tf_op jit(solution)/shard_map/reshape | solution.py:251
  108.8 2.5 %collective-permute-start.6 = (bf16[224,768]{1,0:T(8,128)(2,1)S(1)}, bf16[224,768]{1,0:T(8,128)(2,1)S(1)}, u32[]{:S(2)}, u32[]{:S(2)}) collective-permute-start(bf16[224,768]{1,0:T(8,128)(2,1)S(1)} %gather_fusion.4), channel_id=1, source_target_pairs={{0,3},{1,0},{2,1},{3,2},{4,7},{5,4},{6,5},{7,6},{8,11},{9,8},{10,9... | collective-permute-start | bytes 1032200 | tf_op jit(solution)/shard_map/ppermute | solution.py:17
  112.8 2.7 %collective-permute-start.4 = (bf16[112,1536]{1,0:T(8,128)(2,1)}, bf16[112,1536]{1,0:T(8,128)(2,1)}, u32[]{:S(2)}, u32[]{:S(2)}) collective-permute-start(bf16[112,1536]{1,0:T(8,128)(2,1)} %slice.47), channel_id=1, source_target_pairs={{0,3},{1,0},{2,1},{3,2},{4,7},{5,4},{6,5},{7,6},{8,11},{9,8},{10,9... | collective-permute-start | bytes 1032200 | tf_op jit(solution)/shard_map/ppermute | solution.py:17
  115.5 3.8 %collective-permute-done.5.refs_6_ = bf16[224,768]{1,0:T(8,128)(2,1)S(1)} collective-permute-done((bf16[224,768]{1,0:T(8,128)(2,1)S(1)}, bf16[224,768]{1,0:T(8,128)(2,1)S(1)}, u32[]{:S(2)}, u32[]{:S(2)}) %collective-permute-start.5) | collective-permute-done | bytes 344096 | tf_op jit(solution)/shard_map/ppermute | solution.py:17
  120.6 2.7 %collective-permute-start.8 = (bf16[112,768]{1,0:T(8,128)(2,1)}, bf16[112,768]{1,0:T(8,128)(2,1)}, u32[]{:S(2)}, u32[]{:S(2)}) collective-permute-start(bf16[112,768]{1,0:T(8,128)(2,1)} %slice.49), channel_id=1, source_target_pairs={{0,3},{1,0},{2,1},{3,2},{4,7},{5,4},{6,5},{7,6},{8,11},{9,8},{10,9... | collective-permute-start | bytes 516104 | tf_op jit(solution)/shard_map/ppermute | solution.py:17
  124.8 5.6 %collective-permute-done.7.refs_8_ = bf16[112,768]{1,0:T(8,128)(2,1)} collective-permute-done((bf16[112,768]{1,0:T(8,128)(2,1)}, bf16[112,768]{1,0:T(8,128)(2,1)}, u32[]{:S(2)}, u32[]{:S(2)}) %collective-permute-start.7) | collective-permute-done | bytes 172064 | tf_op jit(solution)/shard_map/ppermute | solution.py:17
  130.3 6.1 %shard_map.91.normed_ref = bf16[4,224,2304]{2,1,0:T(8,128)(2,1)S(1)} custom-call(s32[3]{0:T(128)S(1)} %pad_add_fusion.pos_ref, bf16[224,1536]{1,0:T(8,128)(2,1)S(1)} %gather_fusion.3, bf16[224,1536]{1,0:T(8,128)(2,1)S(1)} %collective-permute-done.1.refs_1_, bf16[224,1536]{1,0:T(8,128)(2,1)S(1)} %collective-permute-done.2.refs_2_, ...), custom_call_target="tpu_custom_call" | custom-call | flops 41287680 | bytes 16515072 | tf_op jit(solution)/shard_map/pallas_call | solution.py:71
  136.4 2.0 %copy-done.1 = bf16[4,224,2304]{2,1,0:T(8,128)(2,1)} copy-done((bf16[4,224,2304]{2,1,0:T(8,128)(2,1)}, bf16[4,224,2304]{2,1,0:T(8,128)(2,1)S(1)}, u32[]{:S(2)}) %copy-start.1) | copy-done | bytes 4128792
  138.4 13.3 %all-gather.2.cloned.1.call-done.weight_ref = bf16[9216,1152]{1,0:T(8,128)(2,1)} async-done(((bf16[144,1152]{1,0:T(8,128)(2,1)}), bf16[9216,1152]{1,0:T(8,128)(2,1)}) %all-gather.2.cloned.1.call-update) | async-done | bytes 21233680 | tf_op jit(solution)/shard_map/all_gather | solution.py:247
  151.8 11.6 %shard_map.92.own = bf16[224,384]{1,0:T(8,128)(2,1)} custom-call(bf16[4,224,2304]{2,1,0:T(8,128)(2,1)} %copy-done.1, bf16[9216,1152]{1,0:T(8,128)(2,1)} %all-gather.2.cloned.1.call-done.weight_ref, f32[1,768]{1,0:T(1,128)} %broadcast_in_dim.18.scale_ref, s32[224,1]{1,0:T(8,128)} %copy.10.seg_col_ref, s32[1,224]{1,0:T(1,128)} %seg_row_ref.1), custom_call_target="tpu_custom_call" | custom-call | flops 3170893824 | bytes 18284544 | tf_op jit(solution)/shard_map/pallas_call | solution.py:139
  163.9 2.2 %collective-permute-start.11 = (bf16[224,384]{1,0:T(8,128)(2,1)}, bf16[224,384]{1,0:T(8,128)(2,1)S(1)}, u32[]{:S(2)}, u32[]{:S(2)}) collective-permute-start(bf16[224,384]{1,0:T(8,128)(2,1)} %shard_map.92.own), channel_id=1, source_target_pairs={{0,3},{1,0},{2,1},{3,2},{4,7},{5,4},{6,5},{7,6},{8,11},{9,8},{10,9... | collective-permute-start | bytes 516104 | tf_op jit(solution)/shard_map/ppermute | solution.py:17
  166.1 4.0 %slice.35 = bf16[9216,384]{1,0:T(8,128)(2,1)S(1)} slice(bf16[9216,1152]{1,0:T(8,128)(2,1)} %all-gather.2.cloned.1.call-done.weight_ref), slice={[0:9216], [768:1152]} | slice | bytes 14155776 | tf_op jit(solution)/shard_map/slice | solution.py:267
  170.7 2.7 %collective-permute-start.12 = (bf16[112,384]{1,0:T(8,128)(2,1)S(1)}, bf16[112,384]{1,0:T(8,128)(2,1)S(1)}, u32[]{:S(2)}, u32[]{:S(2)}) collective-permute-start(bf16[112,384]{1,0:T(8,128)(2,1)S(1)} %slice.51), channel_id=1, source_target_pairs={{0,3},{1,0},{2,1},{3,2},{4,7},{5,4},{6,5},{7,6},{8,11},{9,8},{10,9... | collective-permute-start | bytes 258056 | tf_op jit(solution)/shard_map/ppermute | solution.py:17
  173.4 2.4 %shard_map.93.near = f32[224,2304]{1,0:T(8,128)S(1)} custom-call(s32[3]{0:T(128)S(1)} %pad_add_fusion.pos_ref, bf16[224,384]{1,0:T(8,128)(2,1)S(1)} %copy-done.2, bf16[224,384]{1,0:T(8,128)(2,1)S(1)} %collective-permute-done.9.below, bf16[224,384]{1,0:T(8,128)(2,1)S(1)} %collective-permute-done.11.above, bf16[4,2304,384]{2,1,0:T(8,128)(2,1)S(1)} %bitcast.15), custom_call_target="tpu_custom_call" | custom-call | flops 1189085184 | bytes 8388608 | tf_op jit(solution)/shard_map/pallas_call | solution.py:190
  175.9 2.3 %shard_map.94 = bf16[224,2304]{1,0:T(8,128)(2,1)} custom-call(s32[3]{0:T(128)S(1)} %pad_add_fusion.pos_ref, bf16[112,384]{1,0:T(8,128)(2,1)S(1)} %collective-permute-done.10.low, bf16[112,384]{1,0:T(8,128)(2,1)S(1)} %collective-permute-done.12.high, bf16[4,2304,384]{2,1,0:T(8,128)(2,1)S(1)} %bitcast.16, f32[224,2304]{1,0:T(8,128)S(1)} %shard_map.93.near, ...), custom_call_target="tpu_custom_call" | custom-call | flops 396361728 | bytes 8388608 | tf_op jit(solution)/shard_map/pallas_call | solution.py:190
  (65 shorter events, 10.7 us)
Async XLA Ops:
  6.5 76.6 %copy-start = (s32[1,64]{1,0:T(1,128)S(1)}, s32[1,64]{1,0:T(1,128)}, u32[]{:S(2)}) copy-start(s32[1,64]{1,0:T(1,128)} %param.12) | copy-start | bytes 772
  6.5 145.2 %all-gather.2.cloned.1.call-start = ((), (), s32[]{:S(2)}) async-start(), calls=%async_computation.2 | async-start | bytes 21565440 | tf_op jit(solution)/shard_map/all_gather | solution.py:247
  6.5 9.4 %collective-permute-start = (bf16[144,384]{1,0:T(8,128)(2,1)}, bf16[144,384]{1,0:T(8,128)(2,1)S(1)}, u32[]{:S(2)}, u32[]{:S(2)}) collective-permute-start(bf16[144,384]{1,0:T(8,128)(2,1)} %bitcast.23), channel_id=1, source_target_pairs={{0,0},{1,64},{2,128},{3,192},{32,32},{33,96},{34,160},{35,224},{64... | collective-permute-start | bytes 331784 | tf_op jit(solution)/shard_map/ppermute | solution.py:225
  10.3 3.0 %copy-start.4 = (bf16[64,3,2,768]{3,2,1,0:T(2,128)(2,1)S(1)}, bf16[64,3,2,768]{3,2,1,0:T(2,128)(2,1)}, u32[]{:S(2)}) copy-start(bf16[64,3,2,768]{3,2,1,0:T(2,128)(2,1)} %reshape.75) | copy-start | bytes 1769476
  13.4 2.6 %copy-start.6 = (bf16[144,768]{1,0:T(8,128)(2,1)S(1)}, bf16[144,768]{1,0:T(8,128)(2,1)}, u32[]{:S(2)}) copy-start(bf16[144,768]{1,0:T(8,128)(2,1)} %param.14) | copy-start | bytes 663556
  75.8 7.4 %copy-start.7 = (s32[1,224]{1,0:T(1,128)S(1)}, s32[1,224]{1,0:T(1,128)}, u32[]{:S(2)}) copy-start(s32[1,224]{1,0:T(1,128)} %seg_row_ref.1) | copy-start | bytes 2692
  75.8 29.7 %all-to-all-start.1 = ((bf16[64,3,2,768]{3,2,1,0:T(2,128)(2,1)}), bf16[64,3,2,768]{3,2,1,0:T(2,128)(2,1)}, u32[]{:S(2)}, u32[]{:S(2)}) async-start(bf16[64,3,2,768]{3,2,1,0:T(2,128)(2,1)} %gather_fusion.1), calls=%async_computation.1 | async-start | bytes 1179648 | tf_op jit(solution)/shard_map/all_to_all | solution.py:250
  86.8 24.5 %collective-permute-start.1 = (bf16[224,1536]{1,0:T(8,128)(2,1)S(1)}, bf16[224,1536]{1,0:T(8,128)(2,1)S(1)}, u32[]{:S(2)}, u32[]{:S(2)}) collective-permute-start(bf16[224,1536]{1,0:T(8,128)(2,1)S(1)} %gather_fusion.3), channel_id=1, source_target_pairs={{0,1},{1,2},{2,3},{3,0},{4,5},{5,6},{6,7},{7,4},{8,9},{9,10},{10,1... | collective-permute-start | bytes 2064392 | tf_op jit(solution)/shard_map/ppermute | solution.py:17
  87.1 25.0 %collective-permute-start.2 = (bf16[224,1536]{1,0:T(8,128)(2,1)S(1)}, bf16[224,1536]{1,0:T(8,128)(2,1)S(1)}, u32[]{:S(2)}, u32[]{:S(2)}) collective-permute-start(bf16[224,1536]{1,0:T(8,128)(2,1)S(1)} %gather_fusion.3), channel_id=1, source_target_pairs={{0,3},{1,0},{2,1},{3,2},{4,7},{5,4},{6,5},{7,6},{8,11},{9,8},{10,9... | collective-permute-start | bytes 2064392 | tf_op jit(solution)/shard_map/ppermute | solution.py:17
  108.5 15.6 %copy-start.9 = (f32[768]{0:T(1024)S(1)}, f32[768]{0:T(1024)}, u32[]{:S(2)}) copy-start(f32[768]{0:T(1024)} %param.15) | copy-start | bytes 9220
  108.5 21.8 %copy-start.3 = (f32[9216]{0:T(1024)S(1)}, f32[9216]{0:T(1024)}, u32[]{:S(2)}) copy-start(f32[9216]{0:T(1024)} %param.13) | copy-start | bytes 110596
  108.5 10.7 %collective-permute-start.5 = (bf16[224,768]{1,0:T(8,128)(2,1)S(1)}, bf16[224,768]{1,0:T(8,128)(2,1)S(1)}, u32[]{:S(2)}, u32[]{:S(2)}) collective-permute-start(bf16[224,768]{1,0:T(8,128)(2,1)S(1)} %gather_fusion.4), channel_id=1, source_target_pairs={{0,1},{1,2},{2,3},{3,0},{4,5},{5,6},{6,7},{7,4},{8,9},{9,10},{10,1... | collective-permute-start | bytes 1032200 | tf_op jit(solution)/shard_map/ppermute | solution.py:17
  108.8 11.1 %collective-permute-start.6 = (bf16[224,768]{1,0:T(8,128)(2,1)S(1)}, bf16[224,768]{1,0:T(8,128)(2,1)S(1)}, u32[]{:S(2)}, u32[]{:S(2)}) collective-permute-start(bf16[224,768]{1,0:T(8,128)(2,1)S(1)} %gather_fusion.4), channel_id=1, source_target_pairs={{0,3},{1,0},{2,1},{3,2},{4,7},{5,4},{6,5},{7,6},{8,11},{9,8},{10,9... | collective-permute-start | bytes 1032200 | tf_op jit(solution)/shard_map/ppermute | solution.py:17
  112.1 18.3 %collective-permute-start.3 = (bf16[112,1536]{1,0:T(8,128)(2,1)}, bf16[112,1536]{1,0:T(8,128)(2,1)S(1)}, u32[]{:S(2)}, u32[]{:S(2)}) collective-permute-start(bf16[112,1536]{1,0:T(8,128)(2,1)} %slice.46), channel_id=1, source_target_pairs={{0,1},{1,2},{2,3},{3,0},{4,5},{5,6},{6,7},{7,4},{8,9},{9,10},{10,1... | collective-permute-start | bytes 1032200 | tf_op jit(solution)/shard_map/ppermute | solution.py:17
  112.8 17.5 %collective-permute-start.4 = (bf16[112,1536]{1,0:T(8,128)(2,1)}, bf16[112,1536]{1,0:T(8,128)(2,1)}, u32[]{:S(2)}, u32[]{:S(2)}) collective-permute-start(bf16[112,1536]{1,0:T(8,128)(2,1)} %slice.47), channel_id=1, source_target_pairs={{0,3},{1,0},{2,1},{3,2},{4,7},{5,4},{6,5},{7,6},{8,11},{9,8},{10,9... | collective-permute-start | bytes 1032200 | tf_op jit(solution)/shard_map/ppermute | solution.py:17
  120.0 10.4 %collective-permute-start.7 = (bf16[112,768]{1,0:T(8,128)(2,1)}, bf16[112,768]{1,0:T(8,128)(2,1)}, u32[]{:S(2)}, u32[]{:S(2)}) collective-permute-start(bf16[112,768]{1,0:T(8,128)(2,1)} %slice.48), channel_id=1, source_target_pairs={{0,1},{1,2},{2,3},{3,0},{4,5},{5,6},{6,7},{7,4},{8,9},{9,10},{10,1... | collective-permute-start | bytes 516104 | tf_op jit(solution)/shard_map/ppermute | solution.py:17
  120.6 9.7 %collective-permute-start.8 = (bf16[112,768]{1,0:T(8,128)(2,1)}, bf16[112,768]{1,0:T(8,128)(2,1)}, u32[]{:S(2)}, u32[]{:S(2)}) collective-permute-start(bf16[112,768]{1,0:T(8,128)(2,1)} %slice.49), channel_id=1, source_target_pairs={{0,3},{1,0},{2,1},{3,2},{4,7},{5,4},{6,5},{7,6},{8,11},{9,8},{10,9... | collective-permute-start | bytes 516104 | tf_op jit(solution)/shard_map/ppermute | solution.py:17
  136.4 2.0 %copy-start.1 = (bf16[4,224,2304]{2,1,0:T(8,128)(2,1)}, bf16[4,224,2304]{2,1,0:T(8,128)(2,1)S(1)}, u32[]{:S(2)}) copy-start(bf16[4,224,2304]{2,1,0:T(8,128)(2,1)S(1)} %shard_map.91.normed_ref) | copy-start | bytes 12386308
  138.4 27.7 %copy-start.8 = (f32[2304]{0:T(1024)S(1)}, f32[2304]{0:T(1024)}, u32[]{:S(2)}) copy-start(f32[2304]{0:T(1024)} %param.17) | copy-start | bytes 27652
  163.3 7.2 %collective-permute-start.9 = (bf16[224,384]{1,0:T(8,128)(2,1)}, bf16[224,384]{1,0:T(8,128)(2,1)S(1)}, u32[]{:S(2)}, u32[]{:S(2)}) collective-permute-start(bf16[224,384]{1,0:T(8,128)(2,1)} %shard_map.92.own), channel_id=1, source_target_pairs={{0,1},{1,2},{2,3},{3,0},{4,5},{5,6},{6,7},{7,4},{8,9},{9,10},{10,1... | collective-permute-start | bytes 516104 | tf_op jit(solution)/shard_map/ppermute | solution.py:17
  163.9 6.7 %collective-permute-start.11 = (bf16[224,384]{1,0:T(8,128)(2,1)}, bf16[224,384]{1,0:T(8,128)(2,1)S(1)}, u32[]{:S(2)}, u32[]{:S(2)}) collective-permute-start(bf16[224,384]{1,0:T(8,128)(2,1)} %shard_map.92.own), channel_id=1, source_target_pairs={{0,3},{1,0},{2,1},{3,2},{4,7},{5,4},{6,5},{7,6},{8,11},{9,8},{10,9... | collective-permute-start | bytes 516104 | tf_op jit(solution)/shard_map/ppermute | solution.py:17
  166.1 7.3 %copy-start.2 = (bf16[224,384]{1,0:T(8,128)(2,1)S(1)}, bf16[224,384]{1,0:T(8,128)(2,1)}, u32[]{:S(2)}) copy-start(bf16[224,384]{1,0:T(8,128)(2,1)} %shard_map.92.own) | copy-start | bytes 516100
  170.6 5.3 %collective-permute-start.10 = (bf16[112,384]{1,0:T(8,128)(2,1)S(1)}, bf16[112,384]{1,0:T(8,128)(2,1)S(1)}, u32[]{:S(2)}, u32[]{:S(2)}) collective-permute-start(bf16[112,384]{1,0:T(8,128)(2,1)S(1)} %slice.50), channel_id=1, source_target_pairs={{0,1},{1,2},{2,3},{3,0},{4,5},{5,6},{6,7},{7,4},{8,9},{9,10},{10,1... | collective-permute-start | bytes 258056 | tf_op jit(solution)/shard_map/ppermute | solution.py:17
  170.7 5.2 %collective-permute-start.12 = (bf16[112,384]{1,0:T(8,128)(2,1)S(1)}, bf16[112,384]{1,0:T(8,128)(2,1)S(1)}, u32[]{:S(2)}, u32[]{:S(2)}) collective-permute-start(bf16[112,384]{1,0:T(8,128)(2,1)S(1)} %slice.51), channel_id=1, source_target_pairs={{0,3},{1,0},{2,1},{3,2},{4,7},{5,4},{6,5},{7,6},{8,11},{9,8},{10,9... | collective-permute-start | bytes 258056 | tf_op jit(solution)/shard_map/ppermute | solution.py:17
  (4 other events, 4.5 us)
Sparse Core Ops, SparseCore 0:
  16.9 134.8 all-gather.1
